TPU v7x, 32 devices: a whole 2x2x4 slice. The times are simulated.
32 devices in a mesh: col: 4 (over z), dp: 8 (over y, x, core).
Axes of the slice: x: 2, y: 2, z: 4, core: 2. Of those that a mesh axis runs over, the one named last changes fastest.
Arguments:
- stem_map: bfloat16 [48, 16, 16, 256], P('dp'), may hold values from -6 to 6
- last_one: float32 [48, 16, 16, 256], P('dp'), may hold values from -6 to 6
- last_two: float32 [48, 8, 8, 512], P('dp'), may hold values from -6 to 6
- teach_one: bfloat16 [48, 16, 16, 256], P('dp'), may hold values from -6 to 6
- teach_two: bfloat16 [48, 8, 8, 512], P('dp'), may hold values from -6 to 6
- teacher_slot: int32 [48], P('dp'), may hold values from 0 to 5, as said below
- depth_one: bfloat16 [4, 49, 256], P('col'), may hold values from -0.875 to 0.875
- gains_one: float32 [4, 3, 256], P('col'), may hold values from 0.75 to 1.25
- inner_one: bfloat16 [4, 256, 1024], P('col'), may hold values from -0.375 to 0.375
- outer_one: bfloat16 [4, 1024, 256], P('col'), may hold values from -0.1875 to 0.1875
- depth_two: bfloat16 [4, 49, 512], P('col'), may hold values from -0.875 to 0.875
- gains_two: float32 [4, 3, 512], P('col'), may hold values from 0.75 to 1.25
- inner_two: bfloat16 [4, 512, 2048], P('col'), may hold values from -0.25 to 0.25
- outer_two: bfloat16 [4, 2048, 512], P('col'), may hold values from -0.125 to 0.125
- down_proj: bfloat16 [4, 1024, 512], P('col'), may hold values from -0.1875 to 0.1875
- up_proj: bfloat16 [4, 512, 256], P('col'), may hold values from -0.25 to 0.25
Outputs:
- grad_depth_one: float32 [4, 49, 256], P('col')
- grad_gains_one: float32 [4, 3, 256], P('col')
- grad_inner_one: float32 [4, 256, 1024], P('col')
- grad_outer_one: float32 [4, 1024, 256], P('col')
- grad_depth_two: float32 [4, 49, 512], P('col')
- grad_gains_two: float32 [4, 2, 512], P('col')
- grad_rev_two: float32 [4, 512], P('col')
- grad_inner_two: float32 [4, 512, 2048], P('col')
- grad_outer_two: float32 [4, 2048, 512], P('col')
- grad_down: float32 [4, 1024, 512], P('col')
- grad_up: float32 [4, 512, 256], P('col')
- stem_grad: float32 [48, 16, 16, 256], P('dp')
Inputs may be any that keep to these rules, and one draw needn't show every extreme that they name: `teacher_slot`: each aligned block of 6 entries (the pages of one device) is a permutation of 0 to 5.
All inputs are finite; a program needn't handle non-finite values.
Results may differ from a plain program's by a relative error of at most 0.02.
Values sent between devices are 32-bit elements; how exact they have to be, the bound alone decides.
No kernel may reach another device: no remote copies, remote signals or barrier semaphores. Data moves between devices by JAX's collectives and lax.ppermute only.
A program may use at most 128 MiB of HBM per device.

v0:
```python
import jax
import jax.numpy as jnp
from jax import lax
from jax.sharding import PartitionSpec as P


def passed_along(block, axis, distance):
    devices = range(lax.axis_size(axis))
    route = [(i - distance, i) for i in devices if i - distance in devices]
    return lax.ppermute(block, axis, route)


def depthwise(field_in, kernel_taps):
    side_cells = field_in.shape[1]
    padded = jnp.pad(field_in, ((0, 0), (3, 3), (3, 3), (0, 0)))
    running = jnp.zeros(field_in.shape, jnp.float32)
    for row_offset in range(7):
        for col_offset in range(7):
            running = (
                running
                + padded[
                    :, row_offset : row_offset + side_cells, col_offset : col_offset + side_cells, :
                ]
                * kernel_taps[7 * row_offset + col_offset]
            )
    return running


def norm_part(field_in, kernel_taps, gain_row):
    hidden = depthwise(field_in, kernel_taps)
    center = hidden - jnp.mean(hidden, axis=-1, keepdims=True)
    spread = jnp.mean(center * center, axis=-1, keepdims=True)
    return center * lax.rsqrt(spread + 1e-06) * gain_row


def patchify(field_in):
    page_count, side_cells, _, channels = field_in.shape
    half_side = side_cells // 2
    shaped = field_in.reshape(page_count, half_side, 2, half_side, 2, channels)
    return shaped.transpose(0, 1, 3, 2, 4, 5).reshape(
        page_count, half_side, half_side, 4 * channels
    )


def unpatch(field_in):
    page_count, half_side, _, width_all = field_in.shape
    channels = width_all // 4
    shaped = field_in.reshape(page_count, half_side, half_side, 2, 2, channels)
    return shaped.transpose(0, 1, 3, 2, 4, 5).reshape(
        page_count, 2 * half_side, 2 * half_side, channels
    )


def doubled(field_in):
    return jnp.repeat(jnp.repeat(field_in, 2, axis=1), 2, axis=2)


def pooled(field_in):
    page_count, side_cells, _, channels = field_in.shape
    shaped = field_in.reshape(page_count, side_cells // 2, 2, side_cells // 2, 2, channels)
    return jnp.sum(shaped, axis=(2, 4))


def contract(left_side, right_side):
    left_flat = left_side.reshape(-1, left_side.shape[-1])
    right_flat = right_side.reshape(-1, right_side.shape[-1])
    return lax.dot_general(
        left_flat, right_flat, (((0,), (0,)), ((), ())), preferred_element_type=jnp.float32
    )


def block_forward(field_in, depth, gains, inner, outer):
    normed = norm_part(field_in, depth.astype(jnp.float32), gains[0]).astype(jnp.bfloat16)
    pre_act = jnp.dot(normed, inner, preferred_element_type=jnp.float32)
    activation = jax.nn.gelu(pre_act).astype(jnp.bfloat16)
    block_out = jnp.dot(activation, outer, preferred_element_type=jnp.float32)
    return (gains[1] * block_out, (normed, pre_act, activation, block_out))


def block_backward(field_in, depth, gains, inner, outer, saved, grad_rise):
    normed, pre_act, activation, block_out = saved
    scale_grad = jnp.sum(grad_rise * block_out, axis=(0, 1, 2))
    grad_out = (grad_rise * gains[1]).astype(jnp.bfloat16)
    outer_grad = contract(activation, grad_out)
    grad_act = jnp.dot(grad_out, outer.T, preferred_element_type=jnp.float32)
    _, gelu_back = jax.vjp(jax.nn.gelu, pre_act)
    grad_pre = gelu_back(grad_act)[0].astype(jnp.bfloat16)
    inner_grad = contract(normed, grad_pre)
    grad_norm = jnp.dot(grad_pre, inner.T, preferred_element_type=jnp.float32)
    _, norm_back = jax.vjp(norm_part, field_in, depth.astype(jnp.float32), gains[0])
    field_grad, depth_grad, gain_grad = norm_back(grad_norm)
    return (field_grad, depth_grad, gain_grad, scale_grad, inner_grad, outer_grad)


def column_back(stem_part, high_one, high_two, grad_one, grad_two, weights):
    (
        depth_one,
        gains_one,
        inner_one,
        outer_one,
        depth_two,
        gains_two,
        inner_two,
        outer_two,
        down_proj,
        up_proj,
    ) = weights
    patches = patchify(high_one).astype(jnp.bfloat16)
    lowered = jnp.dot(patches, down_proj, preferred_element_type=jnp.float32)
    rise_two, saved_two = block_forward(lowered, depth_two, gains_two, inner_two, outer_two)
    prev_two = (high_two - rise_two) / gains_two[2]
    coarse = prev_two.astype(jnp.bfloat16)
    entry_field = stem_part.astype(jnp.float32) + doubled(
        jnp.dot(coarse, up_proj, preferred_element_type=jnp.float32)
    )
    rise_one, saved_one = block_forward(entry_field, depth_one, gains_one, inner_one, outer_one)
    prev_one = (high_one - rise_one) / gains_one[2]
    gamma_two = jnp.sum(grad_two * prev_two, axis=(0, 1, 2))
    grad_low, depth_two_g, norm_two_g, scale_two_g, inner_two_g, outer_two_g = block_backward(
        lowered, depth_two, gains_two, inner_two, outer_two, saved_two, grad_two
    )
    low_rounded = grad_low.astype(jnp.bfloat16)
    down_grad = contract(patches, low_rounded)
    total_one = grad_one + unpatch(
        jnp.dot(low_rounded, down_proj.T, preferred_element_type=jnp.float32)
    )
    gamma_one = jnp.sum(total_one * prev_one, axis=(0, 1, 2))
    grad_entry, depth_one_g, norm_one_g, scale_one_g, inner_one_g, outer_one_g = block_backward(
        entry_field, depth_one, gains_one, inner_one, outer_one, saved_one, total_one
    )
    pool_rounded = pooled(grad_entry).astype(jnp.bfloat16)
    up_grad = contract(coarse, pool_rounded)
    next_two = gains_two[2] * grad_two + jnp.dot(
        pool_rounded, up_proj.T, preferred_element_type=jnp.float32
    )
    next_one = gains_one[2] * total_one
    gradients = (
        depth_one_g,
        jnp.stack([norm_one_g, scale_one_g, gamma_one]),
        inner_one_g,
        outer_one_g,
        depth_two_g,
        jnp.stack([norm_two_g, scale_two_g, gamma_two]),
        inner_two_g,
        outer_two_g,
        down_grad,
        up_grad,
    )
    return ((prev_one, prev_two, next_one, next_two), grad_entry, gradients)


def local(
    stem_map,
    last_one,
    last_two,
    teach_one,
    teach_two,
    teacher_slot,
    depth_one,
    gains_one,
    inner_one,
    outer_one,
    depth_two,
    gains_two,
    inner_two,
    outer_two,
    down_proj,
    up_proj,
):
    columns = lax.axis_size("col")
    position = lax.axis_index("col")
    page_count = stem_map.shape[0]
    side_cells = stem_map.shape[1]
    target_one = jnp.take(teach_one, teacher_slot, axis=0).astype(jnp.float32)
    target_two = jnp.take(teach_two, teacher_slot, axis=0).astype(jnp.float32)
    initial = (
        last_one,
        last_two,
        (last_one - target_one) / side_cells,
        (last_two - target_two) / (side_cells // 2),
    )
    weights = tuple(
        (
            w[0]
            for w in (
                depth_one,
                gains_one,
                inner_one,
                outer_one,
                depth_two,
                gains_two,
                inner_two,
                outer_two,
                down_proj,
                up_proj,
            )
        )
    )
    steps_total = columns + page_count - 1
    empty_state = tuple((jnp.zeros((1,) + a.shape[1:], jnp.float32) for a in initial))
    empty_grads = tuple((jnp.zeros(w.shape, jnp.float32) for w in weights))
    empty_stem = jnp.zeros((1,) + stem_map.shape[1:], jnp.float32)

    def advance(step_index, carried):
        received, grad_sums, stem_sums = carried
        micro = step_index - (columns - 1 - position)
        active = jnp.logical_and(micro >= 0, micro < page_count)
        start = jnp.clip(micro, 0, page_count - 1)
        fresh = tuple((lax.dynamic_slice_in_dim(a, start, 1, 0) for a in initial))
        entering = tuple(
            (jnp.where(position == columns - 1, f, r) for f, r in zip(fresh, received))
        )
        page_stem = lax.dynamic_slice_in_dim(stem_map, start, 1, 0)

        def working():
            return column_back(
                page_stem, entering[0], entering[1], entering[2], entering[3], weights
            )

        def resting():
            return (empty_state, empty_stem, empty_grads)

        leaving, entry_grad, gradients = lax.cond(active, working, resting)
        grad_sums = tuple((a + b for a, b in zip(grad_sums, gradients)))
        earlier = lax.dynamic_slice_in_dim(stem_sums, start, 1, 0)
        stem_sums = lax.dynamic_update_slice_in_dim(
            stem_sums, jnp.where(active, entry_grad, earlier), start, 0
        )
        coarse_pair = passed_along((leaving[1], leaving[3]), "col", -1)
        fine_pair = passed_along((leaving[0], leaving[2]), "col", -1)
        received = (fine_pair[0], coarse_pair[0], fine_pair[1], coarse_pair[1])
        return (tuple(received), grad_sums, stem_sums)

    start_carry = (empty_state, empty_grads, jnp.zeros(stem_map.shape, jnp.float32))
    _, grad_sums, stem_sums = lax.fori_loop(0, steps_total, advance, start_carry)
    summed = lax.psum(
        (
            grad_sums[0],
            grad_sums[1],
            grad_sums[2],
            grad_sums[3],
            grad_sums[4],
            grad_sums[5],
            grad_sums[6],
            grad_sums[7],
            grad_sums[8],
            grad_sums[9],
        ),
        "dp",
    )
    stem_total = lax.psum(stem_sums, "col")
    return (
        summed[0][None],
        summed[1][None],
        summed[2][None],
        summed[3][None],
        summed[4][None],
        summed[5][:2][None],
        summed[5][2][None],
        summed[6][None],
        summed[7][None],
        summed[8][None],
        summed[9][None],
        stem_total,
    )


def solution(mesh):
    placed = (
        P("dp", None, None, None),
        P("dp", None, None, None),
        P("dp", None, None, None),
        P("dp", None, None, None),
        P("dp", None, None, None),
        P("dp"),
        P("col", None, None),
        P("col", None, None),
        P("col", None, None),
        P("col", None, None),
        P("col", None, None),
        P("col", None, None),
        P("col", None, None),
        P("col", None, None),
        P("col", None, None),
        P("col", None, None),
    )
    return jax.shard_map(
        local,
        mesh=mesh,
        in_specs=placed,
        out_specs=(
            P("col", None, None),
            P("col", None, None),
            P("col", None, None),
            P("col", None, None),
            P("col", None, None),
            P("col", None, None),
            P("col", None),
            P("col", None, None),
            P("col", None, None),
            P("col", None, None),
            P("col", None, None),
            P("dp", None, None, None),
        ),
        check_vma=False,
    )
```

profile of v0, /device:TPU:0, one launch (start us, length us, event | category | flops | bytes accessed | tf_op | source)
XLA Modules:
  0.0 1094.3 jit_solution(16409008268374883688)
XLA Ops:
  11.5 3.0 subtract_multiply_fusion
  20.9 789.9 %while.44 = (s32[]{:T(128)}, f32[1,16,16,256]{3,2,1,0:T(8,128)}, f32[1,8,8,512]{3,2,1,0:T(8,128)}, f32[1,16,16,256]{3,2,1,0:T(8,128)}, f32[1,8,8,512]{3,2,1,0:T(...) while((s32[]{:T(128)}, f32[1,16,16,256]{3,2,1,0:T(8,128)}, ...), condition=%wide.region_116.117_spmd.clone, body=%wide.region_0.116_spmd.clone.sunk | while | flops 1924810496 | bytes 253962384 | solution.py:235
  21.5 11.7 %conditional.3 = (f32[1,16,16,256]{3,2,1,0:T(8,128)}, f32[1,8,8,512]{3,2,1,0:T(8,128)}, f32[1,16,16,256]{3,2,1,0:T(8,128)}, f32[1,8,8,512]{3,2,1,0:T(8,128)}, f3...) conditional(s32[]{:T(128)} %convert_element_type.198, ...), branch_computations={%region_1.1_spmd, %region_2.115_spmd} | conditional | flops 1918111488 | bytes 135696480 | solution.py:223
  40.1 5.6 select_add_fusion.28
  45.7 3.8 select_add_fusion.29
  59.9 11.7 %conditional.3 = (f32[1,16,16,256]{3,2,1,0:T(8,128)}, f32[1,8,8,512]{3,2,1,0:T(8,128)}, f32[1,16,16,256]{3,2,1,0:T(8,128)}, f32[1,8,8,512]{3,2,1,0:T(8,128)}, f3...) conditional(s32[]{:T(128)} %convert_element_type.198, ...), branch_computations={%region_1.1_spmd, %region_2.115_spmd} | conditional | flops 1918111488 | bytes 135696480 | solution.py:223
  78.6 6.8 select_add_fusion.28
  85.4 3.8 select_add_fusion.29
  99.7 11.7 %conditional.3 = (f32[1,16,16,256]{3,2,1,0:T(8,128)}, f32[1,8,8,512]{3,2,1,0:T(8,128)}, f32[1,16,16,256]{3,2,1,0:T(8,128)}, f32[1,8,8,512]{3,2,1,0:T(8,128)}, f3...) conditional(s32[]{:T(128)} %convert_element_type.198, ...), branch_computations={%region_1.1_spmd, %region_2.115_spmd} | conditional | flops 1918111488 | bytes 135696480 | solution.py:223
  118.3 6.8 select_add_fusion.28
  125.1 3.8 select_add_fusion.29
  138.1 128.0 %collective-permute-done.1 = f32[1,8,8,512]{3,2,1,0:T(8,128)S(1)} collective-permute-done((f32[1,8,8,512]{3,2,1,0:T(8,128)}, f32[1,8,8,512]{3,2,1,0:T(8,128)S(1)}, u32[]{:S(2)}, u32[]{:S(2)}) %collective-permute-start.1) | collective-permute-done | bytes 131104 | tf_op jit(solution)/shard_map/while/body/eval_jaxpr/ppermute | solution.py:10
  268.8 60.3 %conditional.3 = (f32[1,16,16,256]{3,2,1,0:T(8,128)}, f32[1,8,8,512]{3,2,1,0:T(8,128)}, f32[1,16,16,256]{3,2,1,0:T(8,128)}, f32[1,8,8,512]{3,2,1,0:T(8,128)}, f3...) conditional(s32[]{:T(128)} %convert_element_type.198, ...), branch_computations={%region_1.1_spmd, %region_2.115_spmd} | conditional | flops 1918111488 | bytes 135696480 | solution.py:223
  279.3 2.8 fusion.44
  300.3 3.1 fusion.34
  325.6 3.4 convolution_bitcast_fusion
  336.0 6.8 select_add_fusion.28
  342.8 3.8 select_add_fusion.29
  359.6 60.3 %conditional.3 = (f32[1,16,16,256]{3,2,1,0:T(8,128)}, f32[1,8,8,512]{3,2,1,0:T(8,128)}, f32[1,16,16,256]{3,2,1,0:T(8,128)}, f32[1,8,8,512]{3,2,1,0:T(8,128)}, f3...) conditional(s32[]{:T(128)} %convert_element_type.198, ...), branch_computations={%region_1.1_spmd, %region_2.115_spmd} | conditional | flops 1918111488 | bytes 135696480 | solution.py:223
  370.1 2.8 fusion.44
  391.1 3.1 fusion.34
  416.4 3.4 convolution_bitcast_fusion
  426.8 6.8 select_add_fusion.28
  433.7 3.8 select_add_fusion.29
  450.5 60.3 %conditional.3 = (f32[1,16,16,256]{3,2,1,0:T(8,128)}, f32[1,8,8,512]{3,2,1,0:T(8,128)}, f32[1,16,16,256]{3,2,1,0:T(8,128)}, f32[1,8,8,512]{3,2,1,0:T(8,128)}, f3...) conditional(s32[]{:T(128)} %convert_element_type.198, ...), branch_computations={%region_1.1_spmd, %region_2.115_spmd} | conditional | flops 1918111488 | bytes 135696480 | solution.py:223
  461.0 2.8 fusion.44
  482.0 3.1 fusion.34
  507.3 3.4 convolution_bitcast_fusion
  517.7 6.8 select_add_fusion.28
  524.6 3.8 select_add_fusion.29
  541.3 60.3 %conditional.3 = (f32[1,16,16,256]{3,2,1,0:T(8,128)}, f32[1,8,8,512]{3,2,1,0:T(8,128)}, f32[1,16,16,256]{3,2,1,0:T(8,128)}, f32[1,8,8,512]{3,2,1,0:T(8,128)}, f3...) conditional(s32[]{:T(128)} %convert_element_type.198, ...), branch_computations={%region_1.1_spmd, %region_2.115_spmd} | conditional | flops 1918111488 | bytes 135696480 | solution.py:223
  572.8 3.1 fusion.34
  598.2 3.4 convolution_bitcast_fusion
  608.6 6.8 select_add_fusion.28
  615.4 3.8 select_add_fusion.29
  632.2 60.3 %conditional.3 = (f32[1,16,16,256]{3,2,1,0:T(8,128)}, f32[1,8,8,512]{3,2,1,0:T(8,128)}, f32[1,16,16,256]{3,2,1,0:T(8,128)}, f32[1,8,8,512]{3,2,1,0:T(8,128)}, f3...) conditional(s32[]{:T(128)} %convert_element_type.198, ...), branch_computations={%region_1.1_spmd, %region_2.115_spmd} | conditional | flops 1918111488 | bytes 135696480 | solution.py:223
  663.7 3.1 fusion.34
  689.0 3.4 convolution_bitcast_fusion
  699.4 6.8 select_add_fusion.28
  706.3 3.8 select_add_fusion.29
  723.0 60.3 %conditional.3 = (f32[1,16,16,256]{3,2,1,0:T(8,128)}, f32[1,8,8,512]{3,2,1,0:T(8,128)}, f32[1,16,16,256]{3,2,1,0:T(8,128)}, f32[1,8,8,512]{3,2,1,0:T(8,128)}, f3...) conditional(s32[]{:T(128)} %convert_element_type.198, ...), branch_computations={%region_1.1_spmd, %region_2.115_spmd} | conditional | flops 1918111488 | bytes 135696480 | solution.py:223
  754.5 3.1 fusion.34
  779.9 3.4 convolution_bitcast_fusion
  790.3 6.8 select_add_fusion.28
  797.1 3.8 select_add_fusion.29
  813.3 24.1 %all-reduce.198 = (f32[1,49,256]{2,0,1:T(1,128)}, f32[1,3,256]{2,0,1:T(1,128)}, f32[3,512]{1,0:T(4,128)S(1)}) all-reduce(f32[1,49,256]{2,0,1:T(1,128)S(1)} %broadcast_in_dim.765, f32[1,3,256]{2,0,1:T(1,128)S(1)} %broadcast_in_dim.766, f32[3,512]{1,0:T(4,128)S(1)} %copy-done.131), channel_id=1, replica_groups=mesh['col'=4,'dp'=8] {'dp'}, use_global_device_ids=true, to_apply=%region_117.118 | all-reduce | flops 14848 | bytes 118784 | tf_op jit(solution)/shard_map/psum | solution.py:236
  838.7 46.5 %all-reduce.203.cloned.1.call-done = f32[6,16,16,256]{3,2,1,0:T(8,128)} async-done(((f32[6,16,16,256]{3,2,1,0:T(8,128)}), f32[6,16,16,256]{3,2,1,0:T(8,128)}) %all-reduce.203.cloned.1.call-update) | async-done | bytes 1572880 | tf_op jit(solution)/shard_map/psum | solution.py:251
  885.1 186.7 %all-reduce.205.cloned.1.call-done = (f32[1,256,1024]{2,1,0:T(8,128)}, f32[1,1024,256]{2,1,0:T(8,128)}, f32[1,49,512]{2,0,1:T(1,128)}, f32[1,512,2048]{2,1,0:T(8...) async-done(((f32[1,256,1024]{2,1,0:T(8,128)}, f32[1,1024,256]{2,1,0:T(8,128)}, f32[1,49,512]{2,0,1:T(1,128)}, ...) | async-done | bytes 13207568 | tf_op jit(solution)/shard_map/psum | solution.py:236
  (3382 shorter events, 529.0 us)
Async XLA Ops:
  7.2 877.9 %all-reduce.203.cloned.1.call-start = ((), (), s32[]{:S(2)}) async-start(), calls=%async_computation | async-start | bytes 3145728 | tf_op jit(solution)/shard_map/psum | solution.py:251
  33.2 25.5 %collective-permute-start = (f32[1,16,16,256]{3,2,1,0:T(8,128)}, f32[1,16,16,256]{3,2,1,0:T(8,128)}, u32[]{:S(2)}, u32[]{:S(2)}) collective-permute-start(f32[1,16,16,256]{3,2,1,0:T(8,128)} %get-tuple-element.1715), channel_id=1, source_target_pairs={{8,0},{16,8},{24,16},{9,1},{17,9},{25,17},{10,2},{18,10},{26,18},{... | collective-permute-start | bytes 786440 | tf_op jit(solution)/shard_map/while/body/eval_jaxpr/ppermute | solution.py:10
  34.5 24.2 %collective-permute-start.2 = (f32[1,16,16,256]{3,2,1,0:T(8,128)}, f32[1,16,16,256]{3,2,1,0:T(8,128)}, u32[]{:S(2)}, u32[]{:S(2)}) collective-permute-start(f32[1,16,16,256]{3,2,1,0:T(8,128)} %get-tuple-element.1717), channel_id=1, source_target_pairs={{8,0},{16,8},{24,16},{9,1},{17,9},{25,17},{10,2},{18,10},{26,18},{... | collective-permute-start | bytes 786440 | tf_op jit(solution)/shard_map/while/body/eval_jaxpr/ppermute | solution.py:10
  35.8 22.8 %collective-permute-start.1 = (f32[1,8,8,512]{3,2,1,0:T(8,128)}, f32[1,8,8,512]{3,2,1,0:T(8,128)S(1)}, u32[]{:S(2)}, u32[]{:S(2)}) collective-permute-start(f32[1,8,8,512]{3,2,1,0:T(8,128)} %get-tuple-element.1716), channel_id=1, source_target_pairs={{8,0},{16,8},{24,16},{9,1},{17,9},{25,17},{10,2},{18,10},{26,18},{... | collective-permute-start | bytes 393224 | tf_op jit(solution)/shard_map/while/body/eval_jaxpr/ppermute | solution.py:10
  37.1 21.6 %collective-permute-start.3 = (f32[1,8,8,512]{3,2,1,0:T(8,128)}, f32[1,8,8,512]{3,2,1,0:T(8,128)S(1)}, u32[]{:S(2)}, u32[]{:S(2)}) collective-permute-start(f32[1,8,8,512]{3,2,1,0:T(8,128)} %get-tuple-element.1718), channel_id=1, source_target_pairs={{8,0},{16,8},{24,16},{9,1},{17,9},{25,17},{10,2},{18,10},{26,18},{... | collective-permute-start | bytes 393224 | tf_op jit(solution)/shard_map/while/body/eval_jaxpr/ppermute | solution.py:10
  71.7 26.7 %collective-permute-start = (f32[1,16,16,256]{3,2,1,0:T(8,128)}, f32[1,16,16,256]{3,2,1,0:T(8,128)}, u32[]{:S(2)}, u32[]{:S(2)}) collective-permute-start(f32[1,16,16,256]{3,2,1,0:T(8,128)} %get-tuple-element.1715), channel_id=1, source_target_pairs={{8,0},{16,8},{24,16},{9,1},{17,9},{25,17},{10,2},{18,10},{26,18},{... | collective-permute-start | bytes 786440 | tf_op jit(solution)/shard_map/while/body/eval_jaxpr/ppermute | solution.py:10
  73.0 25.5 %collective-permute-start.2 = (f32[1,16,16,256]{3,2,1,0:T(8,128)}, f32[1,16,16,256]{3,2,1,0:T(8,128)}, u32[]{:S(2)}, u32[]{:S(2)}) collective-permute-start(f32[1,16,16,256]{3,2,1,0:T(8,128)} %get-tuple-element.1717), channel_id=1, source_target_pairs={{8,0},{16,8},{24,16},{9,1},{17,9},{25,17},{10,2},{18,10},{26,18},{... | collective-permute-start | bytes 786440 | tf_op jit(solution)/shard_map/while/body/eval_jaxpr/ppermute | solution.py:10
  74.3 24.1 %collective-permute-start.1 = (f32[1,8,8,512]{3,2,1,0:T(8,128)}, f32[1,8,8,512]{3,2,1,0:T(8,128)S(1)}, u32[]{:S(2)}, u32[]{:S(2)}) collective-permute-start(f32[1,8,8,512]{3,2,1,0:T(8,128)} %get-tuple-element.1716), channel_id=1, source_target_pairs={{8,0},{16,8},{24,16},{9,1},{17,9},{25,17},{10,2},{18,10},{26,18},{... | collective-permute-start | bytes 393224 | tf_op jit(solution)/shard_map/while/body/eval_jaxpr/ppermute | solution.py:10
  75.6 22.8 %collective-permute-start.3 = (f32[1,8,8,512]{3,2,1,0:T(8,128)}, f32[1,8,8,512]{3,2,1,0:T(8,128)S(1)}, u32[]{:S(2)}, u32[]{:S(2)}) collective-permute-start(f32[1,8,8,512]{3,2,1,0:T(8,128)} %get-tuple-element.1718), channel_id=1, source_target_pairs={{8,0},{16,8},{24,16},{9,1},{17,9},{25,17},{10,2},{18,10},{26,18},{... | collective-permute-start | bytes 393224 | tf_op jit(solution)/shard_map/while/body/eval_jaxpr/ppermute | solution.py:10
  111.4 156.1 %collective-permute-start = (f32[1,16,16,256]{3,2,1,0:T(8,128)}, f32[1,16,16,256]{3,2,1,0:T(8,128)}, u32[]{:S(2)}, u32[]{:S(2)}) collective-permute-start(f32[1,16,16,256]{3,2,1,0:T(8,128)} %get-tuple-element.1715), channel_id=1, source_target_pairs={{8,0},{16,8},{24,16},{9,1},{17,9},{25,17},{10,2},{18,10},{26,18},{... | collective-permute-start | bytes 786440 | tf_op jit(solution)/shard_map/while/body/eval_jaxpr/ppermute | solution.py:10
  112.7 154.8 %collective-permute-start.2 = (f32[1,16,16,256]{3,2,1,0:T(8,128)}, f32[1,16,16,256]{3,2,1,0:T(8,128)}, u32[]{:S(2)}, u32[]{:S(2)}) collective-permute-start(f32[1,16,16,256]{3,2,1,0:T(8,128)} %get-tuple-element.1717), channel_id=1, source_target_pairs={{8,0},{16,8},{24,16},{9,1},{17,9},{25,17},{10,2},{18,10},{26,18},{... | collective-permute-start | bytes 786440 | tf_op jit(solution)/shard_map/while/body/eval_jaxpr/ppermute | solution.py:10
  114.0 152.1 %collective-permute-start.1 = (f32[1,8,8,512]{3,2,1,0:T(8,128)}, f32[1,8,8,512]{3,2,1,0:T(8,128)S(1)}, u32[]{:S(2)}, u32[]{:S(2)}) collective-permute-start(f32[1,8,8,512]{3,2,1,0:T(8,128)} %get-tuple-element.1716), channel_id=1, source_target_pairs={{8,0},{16,8},{24,16},{9,1},{17,9},{25,17},{10,2},{18,10},{26,18},{... | collective-permute-start | bytes 393224 | tf_op jit(solution)/shard_map/while/body/eval_jaxpr/ppermute | solution.py:10
  115.3 152.2 %collective-permute-start.3 = (f32[1,8,8,512]{3,2,1,0:T(8,128)}, f32[1,8,8,512]{3,2,1,0:T(8,128)S(1)}, u32[]{:S(2)}, u32[]{:S(2)}) collective-permute-start(f32[1,8,8,512]{3,2,1,0:T(8,128)} %get-tuple-element.1718), channel_id=1, source_target_pairs={{8,0},{16,8},{24,16},{9,1},{17,9},{25,17},{10,2},{18,10},{26,18},{... | collective-permute-start | bytes 393224 | tf_op jit(solution)/shard_map/while/body/eval_jaxpr/ppermute | solution.py:10
  133.4 134.7 %copy-start.218 = (f32[3,256]{1,0:T(4,128)S(1)}, f32[3,256]{1,0:T(4,128)}, u32[]{:S(2)}) copy-start(f32[3,256]{1,0:T(4,128)} %copy-done.217) | copy-start | bytes 9220 | tf_op jit(solution)/shard_map/while
  135.4 132.1 %copy-start.17 = (f32[1024,256]{1,0:T(8,128)}, f32[1024,256]{1,0:T(8,128)S(1)}, u32[]{:S(2)}) copy-start(f32[1024,256]{1,0:T(8,128)S(1)} %select_add_fusion.25) | copy-start | bytes 3145732 | tf_op jit(solution)/shard_map/while
  137.0 130.5 %copy-start.20 = (f32[512,256]{1,0:T(8,128)}, f32[512,256]{1,0:T(8,128)S(1)}, u32[]{:S(2)}) copy-start(f32[512,256]{1,0:T(8,128)S(1)} %select_add_fusion.31) | copy-start | bytes 1572868 | tf_op jit(solution)/shard_map/while
  137.1 130.5 %copy-start.38 = (f32[49,512]{1,0:T(8,128)}, f32[49,512]{1,0:T(8,128)S(1)}, u32[]{:S(2)}) copy-start(f32[49,512]{1,0:T(8,128)S(1)} %select_add_fusion.26) | copy-start | bytes 301060 | tf_op jit(solution)/shard_map/while
  138.0 129.6 %copy-start.46 = (f32[49,256]{1,0:T(8,128)}, f32[49,256]{1,0:T(8,128)S(1)}, u32[]{:S(2)}) copy-start(f32[49,256]{1,0:T(8,128)S(1)} %select_add_fusion.22) | copy-start | bytes 150532 | tf_op jit(solution)/shard_map/while
  138.0 129.5 %copy-start.130 = (f32[3,512]{1,0:T(4,128)}, f32[3,512]{1,0:T(4,128)S(1)}, u32[]{:S(2)}) copy-start(f32[3,512]{1,0:T(4,128)S(1)} %select_add_fusion.27) | copy-start | bytes 18436 | tf_op jit(solution)/shard_map/while
  138.1 129.5 %copy-start.212 = (f32[3,256]{1,0:T(4,128)}, f32[3,256]{1,0:T(4,128)S(1)}, u32[]{:S(2)}) copy-start(f32[3,256]{1,0:T(4,128)S(1)} %select_add_fusion.23) | copy-start | bytes 9220 | tf_op jit(solution)/shard_map/while
  329.1 29.3 %collective-permute-start = (f32[1,16,16,256]{3,2,1,0:T(8,128)}, f32[1,16,16,256]{3,2,1,0:T(8,128)}, u32[]{:S(2)}, u32[]{:S(2)}) collective-permute-start(f32[1,16,16,256]{3,2,1,0:T(8,128)} %get-tuple-element.1715), channel_id=1, source_target_pairs={{8,0},{16,8},{24,16},{9,1},{17,9},{25,17},{10,2},{18,10},{26,18},{... | collective-permute-start | bytes 786440 | tf_op jit(solution)/shard_map/while/body/eval_jaxpr/ppermute | solution.py:10
  330.4 28.0 %collective-permute-start.2 = (f32[1,16,16,256]{3,2,1,0:T(8,128)}, f32[1,16,16,256]{3,2,1,0:T(8,128)}, u32[]{:S(2)}, u32[]{:S(2)}) collective-permute-start(f32[1,16,16,256]{3,2,1,0:T(8,128)} %get-tuple-element.1717), channel_id=1, source_target_pairs={{8,0},{16,8},{24,16},{9,1},{17,9},{25,17},{10,2},{18,10},{26,18},{... | collective-permute-start | bytes 786440 | tf_op jit(solution)/shard_map/while/body/eval_jaxpr/ppermute | solution.py:10
  331.7 25.3 %collective-permute-start.1 = (f32[1,8,8,512]{3,2,1,0:T(8,128)}, f32[1,8,8,512]{3,2,1,0:T(8,128)S(1)}, u32[]{:S(2)}, u32[]{:S(2)}) collective-permute-start(f32[1,8,8,512]{3,2,1,0:T(8,128)} %get-tuple-element.1716), channel_id=1, source_target_pairs={{8,0},{16,8},{24,16},{9,1},{17,9},{25,17},{10,2},{18,10},{26,18},{... | collective-permute-start | bytes 393224 | tf_op jit(solution)/shard_map/while/body/eval_jaxpr/ppermute | solution.py:10
  333.0 25.4 %collective-permute-start.3 = (f32[1,8,8,512]{3,2,1,0:T(8,128)}, f32[1,8,8,512]{3,2,1,0:T(8,128)S(1)}, u32[]{:S(2)}, u32[]{:S(2)}) collective-permute-start(f32[1,8,8,512]{3,2,1,0:T(8,128)} %get-tuple-element.1718), channel_id=1, source_target_pairs={{8,0},{16,8},{24,16},{9,1},{17,9},{25,17},{10,2},{18,10},{26,18},{... | collective-permute-start | bytes 393224 | tf_op jit(solution)/shard_map/while/body/eval_jaxpr/ppermute | solution.py:10
  419.9 29.3 %collective-permute-start = (f32[1,16,16,256]{3,2,1,0:T(8,128)}, f32[1,16,16,256]{3,2,1,0:T(8,128)}, u32[]{:S(2)}, u32[]{:S(2)}) collective-permute-start(f32[1,16,16,256]{3,2,1,0:T(8,128)} %get-tuple-element.1715), channel_id=1, source_target_pairs={{8,0},{16,8},{24,16},{9,1},{17,9},{25,17},{10,2},{18,10},{26,18},{... | collective-permute-start | bytes 786440 | tf_op jit(solution)/shard_map/while/body/eval_jaxpr/ppermute | solution.py:10
  421.2 28.0 %collective-permute-start.2 = (f32[1,16,16,256]{3,2,1,0:T(8,128)}, f32[1,16,16,256]{3,2,1,0:T(8,128)}, u32[]{:S(2)}, u32[]{:S(2)}) collective-permute-start(f32[1,16,16,256]{3,2,1,0:T(8,128)} %get-tuple-element.1717), channel_id=1, source_target_pairs={{8,0},{16,8},{24,16},{9,1},{17,9},{25,17},{10,2},{18,10},{26,18},{... | collective-permute-start | bytes 786440 | tf_op jit(solution)/shard_map/while/body/eval_jaxpr/ppermute | solution.py:10
  422.5 25.3 %collective-permute-start.1 = (f32[1,8,8,512]{3,2,1,0:T(8,128)}, f32[1,8,8,512]{3,2,1,0:T(8,128)S(1)}, u32[]{:S(2)}, u32[]{:S(2)}) collective-permute-start(f32[1,8,8,512]{3,2,1,0:T(8,128)} %get-tuple-element.1716), channel_id=1, source_target_pairs={{8,0},{16,8},{24,16},{9,1},{17,9},{25,17},{10,2},{18,10},{26,18},{... | collective-permute-start | bytes 393224 | tf_op jit(solution)/shard_map/while/body/eval_jaxpr/ppermute | solution.py:10
  423.8 25.4 %collective-permute-start.3 = (f32[1,8,8,512]{3,2,1,0:T(8,128)}, f32[1,8,8,512]{3,2,1,0:T(8,128)S(1)}, u32[]{:S(2)}, u32[]{:S(2)}) collective-permute-start(f32[1,8,8,512]{3,2,1,0:T(8,128)} %get-tuple-element.1718), channel_id=1, source_target_pairs={{8,0},{16,8},{24,16},{9,1},{17,9},{25,17},{10,2},{18,10},{26,18},{... | collective-permute-start | bytes 393224 | tf_op jit(solution)/shard_map/while/body/eval_jaxpr/ppermute | solution.py:10
  510.8 13.8 %copy-start.25 = (f32[49,512]{1,0:T(8,128)}, f32[49,512]{1,0:T(8,128)S(1)}, u32[]{:S(2)}) copy-start(f32[49,512]{1,0:T(8,128)S(1)} %get-tuple-element.1723) | copy-start | bytes 301060 | tf_op jit(solution)/shard_map/while
  510.8 29.3 %collective-permute-start = (f32[1,16,16,256]{3,2,1,0:T(8,128)}, f32[1,16,16,256]{3,2,1,0:T(8,128)}, u32[]{:S(2)}, u32[]{:S(2)}) collective-permute-start(f32[1,16,16,256]{3,2,1,0:T(8,128)} %get-tuple-element.1715), channel_id=1, source_target_pairs={{8,0},{16,8},{24,16},{9,1},{17,9},{25,17},{10,2},{18,10},{26,18},{... | collective-permute-start | bytes 786440 | tf_op jit(solution)/shard_map/while/body/eval_jaxpr/ppermute | solution.py:10
  512.1 28.0 %collective-permute-start.2 = (f32[1,16,16,256]{3,2,1,0:T(8,128)}, f32[1,16,16,256]{3,2,1,0:T(8,128)}, u32[]{:S(2)}, u32[]{:S(2)}) collective-permute-start(f32[1,16,16,256]{3,2,1,0:T(8,128)} %get-tuple-element.1717), channel_id=1, source_target_pairs={{8,0},{16,8},{24,16},{9,1},{17,9},{25,17},{10,2},{18,10},{26,18},{... | collective-permute-start | bytes 786440 | tf_op jit(solution)/shard_map/while/body/eval_jaxpr/ppermute | solution.py:10
  513.4 25.3 %collective-permute-start.1 = (f32[1,8,8,512]{3,2,1,0:T(8,128)}, f32[1,8,8,512]{3,2,1,0:T(8,128)S(1)}, u32[]{:S(2)}, u32[]{:S(2)}) collective-permute-start(f32[1,8,8,512]{3,2,1,0:T(8,128)} %get-tuple-element.1716), channel_id=1, source_target_pairs={{8,0},{16,8},{24,16},{9,1},{17,9},{25,17},{10,2},{18,10},{26,18},{... | collective-permute-start | bytes 393224 | tf_op jit(solution)/shard_map/while/body/eval_jaxpr/ppermute | solution.py:10
  514.7 25.4 %collective-permute-start.3 = (f32[1,8,8,512]{3,2,1,0:T(8,128)}, f32[1,8,8,512]{3,2,1,0:T(8,128)S(1)}, u32[]{:S(2)}, u32[]{:S(2)}) collective-permute-start(f32[1,8,8,512]{3,2,1,0:T(8,128)} %get-tuple-element.1718), channel_id=1, source_target_pairs={{8,0},{16,8},{24,16},{9,1},{17,9},{25,17},{10,2},{18,10},{26,18},{... | collective-permute-start | bytes 393224 | tf_op jit(solution)/shard_map/while/body/eval_jaxpr/ppermute | solution.py:10
  601.6 13.8 %copy-start.25 = (f32[49,512]{1,0:T(8,128)}, f32[49,512]{1,0:T(8,128)S(1)}, u32[]{:S(2)}) copy-start(f32[49,512]{1,0:T(8,128)S(1)} %get-tuple-element.1723) | copy-start | bytes 301060 | tf_op jit(solution)/shard_map/while
  601.6 29.3 %collective-permute-start = (f32[1,16,16,256]{3,2,1,0:T(8,128)}, f32[1,16,16,256]{3,2,1,0:T(8,128)}, u32[]{:S(2)}, u32[]{:S(2)}) collective-permute-start(f32[1,16,16,256]{3,2,1,0:T(8,128)} %get-tuple-element.1715), channel_id=1, source_target_pairs={{8,0},{16,8},{24,16},{9,1},{17,9},{25,17},{10,2},{18,10},{26,18},{... | collective-permute-start | bytes 786440 | tf_op jit(solution)/shard_map/while/body/eval_jaxpr/ppermute | solution.py:10
  602.9 28.0 %collective-permute-start.2 = (f32[1,16,16,256]{3,2,1,0:T(8,128)}, f32[1,16,16,256]{3,2,1,0:T(8,128)}, u32[]{:S(2)}, u32[]{:S(2)}) collective-permute-start(f32[1,16,16,256]{3,2,1,0:T(8,128)} %get-tuple-element.1717), channel_id=1, source_target_pairs={{8,0},{16,8},{24,16},{9,1},{17,9},{25,17},{10,2},{18,10},{26,18},{... | collective-permute-start | bytes 786440 | tf_op jit(solution)/shard_map/while/body/eval_jaxpr/ppermute | solution.py:10
  604.2 25.3 %collective-permute-start.1 = (f32[1,8,8,512]{3,2,1,0:T(8,128)}, f32[1,8,8,512]{3,2,1,0:T(8,128)S(1)}, u32[]{:S(2)}, u32[]{:S(2)}) collective-permute-start(f32[1,8,8,512]{3,2,1,0:T(8,128)} %get-tuple-element.1716), channel_id=1, source_target_pairs={{8,0},{16,8},{24,16},{9,1},{17,9},{25,17},{10,2},{18,10},{26,18},{... | collective-permute-start | bytes 393224 | tf_op jit(solution)/shard_map/while/body/eval_jaxpr/ppermute | solution.py:10
  605.5 25.4 %collective-permute-start.3 = (f32[1,8,8,512]{3,2,1,0:T(8,128)}, f32[1,8,8,512]{3,2,1,0:T(8,128)S(1)}, u32[]{:S(2)}, u32[]{:S(2)}) collective-permute-start(f32[1,8,8,512]{3,2,1,0:T(8,128)} %get-tuple-element.1718), channel_id=1, source_target_pairs={{8,0},{16,8},{24,16},{9,1},{17,9},{25,17},{10,2},{18,10},{26,18},{... | collective-permute-start | bytes 393224 | tf_op jit(solution)/shard_map/while/body/eval_jaxpr/ppermute | solution.py:10
  692.5 13.8 %copy-start.25 = (f32[49,512]{1,0:T(8,128)}, f32[49,512]{1,0:T(8,128)S(1)}, u32[]{:S(2)}) copy-start(f32[49,512]{1,0:T(8,128)S(1)} %get-tuple-element.1723) | copy-start | bytes 301060 | tf_op jit(solution)/shard_map/while
  692.5 29.3 %collective-permute-start = (f32[1,16,16,256]{3,2,1,0:T(8,128)}, f32[1,16,16,256]{3,2,1,0:T(8,128)}, u32[]{:S(2)}, u32[]{:S(2)}) collective-permute-start(f32[1,16,16,256]{3,2,1,0:T(8,128)} %get-tuple-element.1715), channel_id=1, source_target_pairs={{8,0},{16,8},{24,16},{9,1},{17,9},{25,17},{10,2},{18,10},{26,18},{... | collective-permute-start | bytes 786440 | tf_op jit(solution)/shard_map/while/body/eval_jaxpr/ppermute | solution.py:10
  693.8 28.0 %collective-permute-start.2 = (f32[1,16,16,256]{3,2,1,0:T(8,128)}, f32[1,16,16,256]{3,2,1,0:T(8,128)}, u32[]{:S(2)}, u32[]{:S(2)}) collective-permute-start(f32[1,16,16,256]{3,2,1,0:T(8,128)} %get-tuple-element.1717), channel_id=1, source_target_pairs={{8,0},{16,8},{24,16},{9,1},{17,9},{25,17},{10,2},{18,10},{26,18},{... | collective-permute-start | bytes 786440 | tf_op jit(solution)/shard_map/while/body/eval_jaxpr/ppermute | solution.py:10
  695.1 25.3 %collective-permute-start.1 = (f32[1,8,8,512]{3,2,1,0:T(8,128)}, f32[1,8,8,512]{3,2,1,0:T(8,128)S(1)}, u32[]{:S(2)}, u32[]{:S(2)}) collective-permute-start(f32[1,8,8,512]{3,2,1,0:T(8,128)} %get-tuple-element.1716), channel_id=1, source_target_pairs={{8,0},{16,8},{24,16},{9,1},{17,9},{25,17},{10,2},{18,10},{26,18},{... | collective-permute-start | bytes 393224 | tf_op jit(solution)/shard_map/while/body/eval_jaxpr/ppermute | solution.py:10
  696.4 25.4 %collective-permute-start.3 = (f32[1,8,8,512]{3,2,1,0:T(8,128)}, f32[1,8,8,512]{3,2,1,0:T(8,128)S(1)}, u32[]{:S(2)}, u32[]{:S(2)}) collective-permute-start(f32[1,8,8,512]{3,2,1,0:T(8,128)} %get-tuple-element.1718), channel_id=1, source_target_pairs={{8,0},{16,8},{24,16},{9,1},{17,9},{25,17},{10,2},{18,10},{26,18},{... | collective-permute-start | bytes 393224 | tf_op jit(solution)/shard_map/while/body/eval_jaxpr/ppermute | solution.py:10
  783.4 26.7 %collective-permute-start = (f32[1,16,16,256]{3,2,1,0:T(8,128)}, f32[1,16,16,256]{3,2,1,0:T(8,128)}, u32[]{:S(2)}, u32[]{:S(2)}) collective-permute-start(f32[1,16,16,256]{3,2,1,0:T(8,128)} %get-tuple-element.1715), channel_id=1, source_target_pairs={{8,0},{16,8},{24,16},{9,1},{17,9},{25,17},{10,2},{18,10},{26,18},{... | collective-permute-start | bytes 786440 | tf_op jit(solution)/shard_map/while/body/eval_jaxpr/ppermute | solution.py:10
  784.7 25.5 %collective-permute-start.2 = (f32[1,16,16,256]{3,2,1,0:T(8,128)}, f32[1,16,16,256]{3,2,1,0:T(8,128)}, u32[]{:S(2)}, u32[]{:S(2)}) collective-permute-start(f32[1,16,16,256]{3,2,1,0:T(8,128)} %get-tuple-element.1717), channel_id=1, source_target_pairs={{8,0},{16,8},{24,16},{9,1},{17,9},{25,17},{10,2},{18,10},{26,18},{... | collective-permute-start | bytes 786440 | tf_op jit(solution)/shard_map/while/body/eval_jaxpr/ppermute | solution.py:10
  786.0 24.1 %collective-permute-start.1 = (f32[1,8,8,512]{3,2,1,0:T(8,128)}, f32[1,8,8,512]{3,2,1,0:T(8,128)S(1)}, u32[]{:S(2)}, u32[]{:S(2)}) collective-permute-start(f32[1,8,8,512]{3,2,1,0:T(8,128)} %get-tuple-element.1716), channel_id=1, source_target_pairs={{8,0},{16,8},{24,16},{9,1},{17,9},{25,17},{10,2},{18,10},{26,18},{... | collective-permute-start | bytes 393224 | tf_op jit(solution)/shard_map/while/body/eval_jaxpr/ppermute | solution.py:10
  787.3 22.8 %collective-permute-start.3 = (f32[1,8,8,512]{3,2,1,0:T(8,128)}, f32[1,8,8,512]{3,2,1,0:T(8,128)S(1)}, u32[]{:S(2)}, u32[]{:S(2)}) collective-permute-start(f32[1,8,8,512]{3,2,1,0:T(8,128)} %get-tuple-element.1718), channel_id=1, source_target_pairs={{8,0},{16,8},{24,16},{9,1},{17,9},{25,17},{10,2},{18,10},{26,18},{... | collective-permute-start | bytes 393224 | tf_op jit(solution)/shard_map/while/body/eval_jaxpr/ppermute | solution.py:10
  810.8 261.0 %all-reduce.205.cloned.1.call-start = ((), (), s32[]{:S(2)}) async-start(), calls=%async_computation.1 | async-start | bytes 26415104 | tf_op jit(solution)/shard_map/psum | solution.py:236
  (1360 other events, 5978.1 us)
Sparse Core Ops, SparseCore 0:
  810.9 74.1 all-reduce.202
  891.2 180.6 all-reduce.204
where the time goes:
time: 1100 us; the launch traced here: 1090 us
  waiting for transfers between devices  376 us (34%)
  other arithmetic  315 us (29%)
  matrix products  163 us (15%)
  local copies, waits for them, and re-layouts  135 us (12%)
  starting transfers between devices  46.6 us (4%)
  blocking collectives  24.1 us (2%)
  loops' own time  21 us (2%)
  between operations  14.2 us (1%)
    psum x1, waiting for transfers between devices, local(): lax.psum((grad_sums[0], grad_sums[1], grad_sums[2], grad_sums[3], grad_su...  187 us
    add x90, other arithmetic, advance(): grad_sums = tuple((a + b for a, b in zip(grad_sums, gradients)))  162 us
    ppermute x36, waiting for transfers between devices, passed_along(): return lax.ppermute(block, axis, route)  142 us
    dot_general x36, matrix products, contract(): lax.dot_general(left_flat, right_flat, (((0,), (0,)), ((), ())), preferre...  76.4 us
    ppermute x36, starting transfers between devices, passed_along(): return lax.ppermute(block, axis, route)  46.5 us
    psum x1, waiting for transfers between devices, local(): stem_total = lax.psum(stem_sums, 'col')  46.5 us
    slice x36, local copies, waits for them, and re-layouts, depthwise(): kernel_taps[7 * row_offset + col_offset]  37.8 us
    dot_general x12, matrix products, block_forward(): block_out = jnp.dot(activation, outer, preferred_element_type=jnp.float32)  35.6 us
  transfers between devices with their start and end apart: 38, of which 14 were waited for; matrix products, arithmetic and copies ran while one was open for 16% of the time, Pallas kernels for 0%

commit v1 on v0

v1 whole, which is shorter than its diff:
```python
import jax
import jax.numpy as jnp
from jax import lax
from jax.experimental import pallas as pl
from jax.experimental.pallas import tpu as pltpu
from jax.sharding import PartitionSpec as P

F32 = jnp.float32
BF16 = jnp.bfloat16
LANES = 128
EPS = 1e-06
G0 = 0.7978845608028654
G1 = 0.044715
NT = (((1,), (1,)), ((), ()))


def shift_rows(block, step):
    if step == 0:
        return block
    rolled = pltpu.roll(block, (-step) % 8, 0)
    place = lax.broadcasted_iota(jnp.int32, block.shape, 0) + step
    return jnp.where((place >= 0) & (place < 8), rolled, 0.0)


def fine_shifts(col_parity):
    return (-1, 0, 1, 2) if col_parity == 0 else (-2, -1, 0, 1)


def fill_fine(shifted, value, phase):
    for row in range(8):
        line = value[8 * row : 8 * row + 8]
        for k, step in enumerate(fine_shifts(phase & 1)):
            shifted[k, phase, 8 * row : 8 * row + 8, :] = shift_rows(line, step)


def fill_coarse(shifted, value):
    for row in range(8):
        line = value[8 * row : 8 * row + 8]
        for k in range(7):
            shifted[k, 8 * row : 8 * row + 8, :] = shift_rows(line, k - 3)


def fine_source(dj, b):
    off = dj + b - 3
    pj = off & 1
    step = (off - pj) // 2
    return pj, step + (1 if pj == 0 else 2)


def conv_fine(shifted, taps, out, flip):
    def lane_block(lb, carry):
        lanes = pl.ds(pl.multiple_of(lb * LANES, LANES), LANES)
        for dj in range(2):
            acc = [None] * 16
            for b in range(7):
                pj, k = fine_source(dj, b)
                w = []
                for a in range(7):
                    t = 48 - (7 * a + b) if flip else 7 * a + b
                    w.append(jnp.broadcast_to(taps[t : t + 1, lanes], (8, LANES)))
                for ip in range(16):
                    r = 8 * (ip >> 1)
                    x = shifted[k, 2 * (ip & 1) + pj, r : r + 8, lanes]
                    for a in range(7):
                        i = ip - (a - 3)
                        if 0 <= i < 16:
                            acc[i] = x * w[a] if acc[i] is None else acc[i] + x * w[a]
            for i in range(16):
                r = 8 * (i >> 1)
                out[2 * (i & 1) + dj, r : r + 8, lanes] = acc[i]
        return carry

    lax.fori_loop(0, shifted.shape[-1] // LANES, lane_block, 0)


def taps_fine(shifted, field, out):
    def lane_block(lb, carry):
        lanes = pl.ds(pl.multiple_of(lb * LANES, LANES), LANES)
        for b in range(7):
            acc = [None] * 7
            for dj in range(2):
                pj, k = fine_source(dj, b)
                v = [
                    field[2 * (i & 1) + dj, 8 * (i >> 1) : 8 * (i >> 1) + 8, lanes]
                    for i in range(16)
                ]
                for ip in range(16):
                    r = 8 * (ip >> 1)
                    x = shifted[k, 2 * (ip & 1) + pj, r : r + 8, lanes]
                    for a in range(7):
                        i = ip - (a - 3)
                        if 0 <= i < 16:
                            acc[a] = x * v[i] if acc[a] is None else acc[a] + x * v[i]
            for a in range(7):
                t = 48 - (7 * a + b)
                out[t : t + 1, lanes] = jnp.sum(acc[a], axis=0, keepdims=True)
        return carry

    lax.fori_loop(0, shifted.shape[-1] // LANES, lane_block, 0)


def conv_coarse(shifted, taps, out, flip):
    def lane_block(lb, carry):
        lanes = pl.ds(pl.multiple_of(lb * LANES, LANES), LANES)
        acc = [None] * 8
        for b in range(7):
            w = []
            for a in range(7):
                t = 48 - (7 * a + b) if flip else 7 * a + b
                w.append(jnp.broadcast_to(taps[t : t + 1, lanes], (8, LANES)))
            for ip in range(8):
                x = shifted[b, 8 * ip : 8 * ip + 8, lanes]
                for a in range(7):
                    i = ip - (a - 3)
                    if 0 <= i < 8:
                        acc[i] = x * w[a] if acc[i] is None else acc[i] + x * w[a]
        for i in range(8):
            out[8 * i : 8 * i + 8, lanes] = acc[i]
        return carry

    lax.fori_loop(0, shifted.shape[-1] // LANES, lane_block, 0)


def taps_coarse(shifted, field, out):
    def lane_block(lb, carry):
        lanes = pl.ds(pl.multiple_of(lb * LANES, LANES), LANES)
        v = [field[8 * i : 8 * i + 8, lanes] for i in range(8)]
        for b in range(7):
            acc = [None] * 7
            for ip in range(8):
                x = shifted[b, 8 * ip : 8 * ip + 8, lanes]
                for a in range(7):
                    i = ip - (a - 3)
                    if 0 <= i < 8:
                        acc[a] = x * v[i] if acc[a] is None else acc[a] + x * v[i]
            for a in range(7):
                t = 48 - (7 * a + b)
                out[t : t + 1, lanes] = jnp.sum(acc[a], axis=0, keepdims=True)
        return carry

    lax.fori_loop(0, shifted.shape[-1] // LANES, lane_block, 0)


def normalise(hidden):
    center = hidden - jnp.mean(hidden, axis=-1, keepdims=True)
    spread = jnp.mean(center * center, axis=-1, keepdims=True)
    scale = lax.rsqrt(spread + EPS)
    return center * scale, scale


def norm_back(grad, unit, scale, gain):
    g = grad * gain
    first = jnp.mean(g, axis=-1, keepdims=True)
    second = jnp.mean(g * unit, axis=-1, keepdims=True)
    return scale * (g - first - unit * second)


def gelu_pair(x):
    x2 = x * x
    t = jnp.tanh(x * (G0 + (G0 * G1) * x2))
    h = 0.5 + 0.5 * t
    act = x * h
    slope = h + act * (1.0 - t) * (G0 + (3.0 * G0 * G1) * x2)
    return act, slope


class Moves:
    def __init__(self, sems):
        self.sems = sems
        self.used = 0
        self.open = []

    def make(self, src, dst):
        copy = pltpu.make_async_copy(src, dst, self.sems.at[self.used])
        self.used += 1
        return copy

    def bring(self, src, dst):
        copy = self.make(src, dst)
        copy.start()
        return copy

    def pick(self, flag, src_if, src_else, dst):
        sem = self.sems.at[self.used]
        self.used += 1

        @pl.when(flag)
        def _():
            pltpu.make_async_copy(src_if, dst, sem).start()

        @pl.when(jnp.logical_not(flag))
        def _():
            pltpu.make_async_copy(src_else, dst, sem).start()

        return pltpu.make_async_copy(src_else, dst, sem)

    def send(self, src, dst):
        copy = self.make(src, dst)
        copy.start()
        self.open.append(copy)

    def finish(self):
        for copy in self.open:
            copy.wait()


def dot(a, b):
    return jnp.dot(a, b, preferred_element_type=F32)


def dot_nt(a, b):
    return lax.dot_general(a, b, NT, preferred_element_type=F32)


def forward_kernel(
    where,
    last1, last2, stem, recv,
    depth1, gains1, inner1, outer1, depth2, gains2, inner2, outer2, down, up,
    *rest,
):
    (
        send, t_two, t_one, t_r2, t_r1, t_d2, t_d1,
        patch, nrm2, act2, coarse, nrm1, act1,
        h1, h2, st, w_in1, w_out1, w_in2, w_out2, w_down, w_up,
        sh1, sh2, two, one, r2, r1, d2, d1,
        v_patch, v_nrm2, v_act2, v_coarse, v_nrm1, v_act1, p1, p2, sems,
    ) = rest[-39:]
    mv = Moves(sems)
    page, spot, first = where[0], where[1], where[2] == 1
    half = h2.shape[-1] // 2
    c_h1 = mv.pick(first, last1.at[page], recv.at[0:4], h1)
    c_h2 = [
        mv.pick(first, last2.at[page, :, half * s : half * s + half], recv.at[4 + s],
                h2.at[:, half * s : half * s + half])
        for s in range(2)
    ]
    c_down = mv.bring(down, w_down)
    c_in2 = mv.bring(inner2, w_in2)
    c_out2 = mv.bring(outer2, w_out2)
    c_up = mv.bring(up, w_up)
    c_st = mv.bring(stem.at[page], st)
    c_in1 = mv.bring(inner1, w_in1)
    c_out1 = mv.bring(outer1, w_out1)
    c1, c2 = h1.shape[-1], h2.shape[-1]

    c_h1.wait()
    c_down.wait()
    low = None
    for q in range(4):
        v_patch[q] = h1[q].astype(BF16)
        part = dot(v_patch[q], w_down[c1 * q : c1 * q + c1, :])
        low = part if low is None else low + part
    mv.send(v_patch, patch.at[spot])
    two[0] = low
    fill_coarse(sh2, low)
    conv_coarse(sh2, depth2, two.at[1], False)
    unit, scale = normalise(two[1])
    two[1] = unit
    r2[...] = jnp.broadcast_to(scale, r2.shape)
    v_nrm2[...] = (unit * gains2[0:1, :]).astype(BF16)
    mv.send(v_nrm2, nrm2.at[spot])
    mv.send(r2, t_r2)
    c_in2.wait()
    wide2 = w_in2.shape[-1]
    for n in range(0, wide2, 512):
        a, s = gelu_pair(dot(v_nrm2[...], w_in2[:, n : n + 512]))
        v_act2[:, n : n + 512] = a.astype(BF16)
        d2[:, n : n + 512] = s.astype(BF16)
    mv.send(v_act2, act2.at[spot])
    mv.send(d2, t_d2)
    c_out2.wait()
    out2 = dot(v_act2[...], w_out2[...])
    two[2] = out2
    for copy in c_h2:
        copy.wait()
    prev2 = (h2[...] - gains2[1:2, :] * out2) / gains2[2:3, :]
    p2[...] = prev2
    mv.send(two, t_two)
    for s in range(2):
        mv.send(p2.at[:, half * s : half * s + half], send.at[4 + s])
    v_coarse[...] = prev2.astype(BF16)
    mv.send(v_coarse, coarse.at[spot])
    c_up.wait()
    lift = dot(v_coarse[...], w_up[...])
    c_st.wait()
    for q in range(4):
        entry = st[q].astype(F32) + lift
        one[0, q] = entry
        fill_fine(sh1, entry, q)
    conv_fine(sh1, depth1, one.at[1], False)
    for q in range(4):
        unit, scale = normalise(one[1, q])
        one[1, q] = unit
        r1[q] = jnp.broadcast_to(scale, r1.shape[1:])
        v_nrm1[64 * q : 64 * q + 64, :] = (unit * gains1[0:1, :]).astype(BF16)
    mv.send(v_nrm1, nrm1.at[spot])
    mv.send(r1, t_r1)
    c_in1.wait()
    wide1 = w_in1.shape[-1]
    for n in range(0, wide1, 256):
        a, s = gelu_pair(dot(v_nrm1[...], w_in1[:, n : n + 256]))
        v_act1[:, n : n + 256] = a.astype(BF16)
        d1[:, n : n + 256] = s.astype(BF16)
    mv.send(v_act1, act1.at[spot])
    mv.send(d1, t_d1)
    c_out1.wait()
    for q in range(4):
        out1 = dot(v_act1[64 * q : 64 * q + 64, :], w_out1[...])
        one[2, q] = out1
        p1[q] = (h1[q] - gains1[1:2, :] * out1) / gains1[2:3, :]
    mv.send(one, t_one)
    mv.send(p1, send.at[0:4])
    mv.finish()


def backward_kernel(
    where,
    last1, last2, teach1, teach2, recv, prev, t_two, t_one, t_r2, t_r1, t_d2, t_d1,
    depth1, gains1, inner1, outer1, depth2, gains2, inner2, outer2, down, up,
    *rest,
):
    (
        send, gout2, gpre2, glow, gout1, gpre1, gpool, stem, small,
        g1, g2, te1, te2, p1, p2, two, one, r2, r1, d2, d1,
        w_in1, w_out1, w_in2, w_out2, w_down, w_up,
        sh1, sh2, low_g, ent_g,
        v_gout2, v_gpre2, v_glow, v_gout1, v_gpre1, v_gpool, v_small, n1, n2,
        sems,
    ) = rest[-41:]
    mv = Moves(sems)
    v_small[...] = jnp.zeros_like(v_small)
    page, spot, first, slot = where[0], where[1], where[2] == 1, where[3]
    half = g2.shape[-1] // 2
    c1, c2 = g1.shape[-1], g2.shape[-1]
    c_g2 = [
        mv.pick(first, last2.at[page, :, half * s : half * s + half], recv.at[4 + s],
                g2.at[:, half * s : half * s + half])
        for s in range(2)
    ]
    c_te2 = mv.bring(teach2.at[slot], te2)
    c_out2 = mv.bring(outer2, w_out2)
    c_d2 = mv.bring(t_d2, d2)
    c_two = mv.bring(t_two, two)
    c_in2 = mv.bring(inner2, w_in2)
    c_r2 = mv.bring(t_r2, r2)
    c_p2 = [mv.bring(prev.at[4 + s], p2.at[:, half * s : half * s + half]) for s in range(2)]
    c_g1 = mv.pick(first, last1.at[page], recv.at[0:4], g1)
    c_te1 = mv.bring(teach1.at[slot], te1)
    c_down = mv.bring(down, w_down)
    c_p1 = mv.bring(prev.at[0:4], p1)
    c_one = mv.bring(t_one, one)
    c_out1 = mv.bring(outer1, w_out1)
    c_d1 = mv.bring(t_d1, d1)
    c_in1 = mv.bring(inner1, w_in1)
    c_r1 = mv.bring(t_r1, r1)
    c_up = mv.bring(up, w_up)

    for copy in c_g2:
        copy.wait()
    c_te2.wait()

    @pl.when(first)
    def _():
        g2[...] = (g2[...] - te2[...].astype(F32)) / 8.0

    v_gout2[...] = (gains2[1:2, :] * g2[...]).astype(BF16)
    mv.send(v_gout2, gout2.at[spot])
    c_out2.wait()
    c_d2.wait()
    wide2 = w_in2.shape[-1]
    for n in range(0, wide2, 512):
        part = dot_nt(v_gout2[...], w_out2[n : n + 512, :])
        v_gpre2[:, n : n + 512] = (part * d2[:, n : n + 512].astype(F32)).astype(BF16)
    mv.send(v_gpre2, gpre2.at[spot])
    c_in2.wait()
    gn = dot_nt(v_gpre2[...], w_in2[...])
    c_two.wait()
    c_r2.wait()
    for copy in c_p2:
        copy.wait()
    unit = two[1]
    v_small[56:57, :] = jnp.sum(gn * unit, axis=0, keepdims=True)
    v_small[57:58, :] = jnp.sum(g2[...] * two[2], axis=0, keepdims=True)
    v_small[58:59, :] = jnp.sum(g2[...] * p2[...], axis=0, keepdims=True)
    fill_coarse(sh2, norm_back(gn, unit, r2[:, 0:1], gains2[0:1, :]))
    conv_coarse(sh2, depth2, low_g, True)
    v_glow[...] = low_g[...].astype(BF16)
    mv.send(v_glow, glow.at[spot])
    taps_coarse(sh2, two.at[0], v_small.at[0:56])
    c_g1.wait()
    c_te1.wait()

    @pl.when(first)
    def _():
        for q in range(4):
            g1[q] = (g1[q] - te1[q].astype(F32)) / 16.0

    c_down.wait()
    c_p1.wait()
    c_one.wait()
    gamma = jnp.zeros((1, c1), F32)
    layer = jnp.zeros((1, c1), F32)
    for q in range(4):
        total = g1[q] + dot_nt(v_glow[...], w_down[c1 * q : c1 * q + c1, :])
        gamma += jnp.sum(total * p1[q], axis=0, keepdims=True)
        layer += jnp.sum(total * one[2, q], axis=0, keepdims=True)
        v_gout1[64 * q : 64 * q + 64, :] = (gains1[1:2, :] * total).astype(BF16)
        n1[q] = gains1[2:3, :] * total
    mv.send(n1, send.at[0:4])
    mv.send(v_gout1, gout1.at[spot])
    c_out1.wait()
    c_d1.wait()
    wide1 = w_in1.shape[-1]
    for n in range(0, wide1, 256):
        part = dot_nt(v_gout1[...], w_out1[n : n + 256, :])
        v_gpre1[:, n : n + 256] = (part * d1[:, n : n + 256].astype(F32)).astype(BF16)
    mv.send(v_gpre1, gpre1.at[spot])
    c_in1.wait()
    c_r1.wait()
    ggain = jnp.zeros((1, c1), F32)
    for q in range(4):
        gn = dot_nt(v_gpre1[64 * q : 64 * q + 64, :], w_in1[...])
        unit = one[1, q]
        ggain += jnp.sum(gn * unit, axis=0, keepdims=True)
        fill_fine(sh1, norm_back(gn, unit, r1[q, :, 0:1], gains1[0:1, :]), q)
    v_small[120:121, 0:c1] = ggain
    v_small[121:122, 0:c1] = layer
    v_small[122:123, 0:c1] = gamma
    conv_fine(sh1, depth1, ent_g, True)
    mv.send(ent_g, stem.at[spot])
    v_gpool[...] = (ent_g[0] + ent_g[1] + ent_g[2] + ent_g[3]).astype(BF16)
    mv.send(v_gpool, gpool.at[spot])
    c_up.wait()
    n2[...] = gains2[2:3, :] * g2[...] + dot_nt(v_gpool[...], w_up[...])
    for s in range(2):
        mv.send(n2.at[:, half * s : half * s + half], send.at[4 + s])
    taps_fine(sh1, one.at[0], v_small.at[64:120, 0:c1])
    mv.send(v_small, small.at[spot])
    mv.finish()


ANY = pl.BlockSpec(memory_space=pl.ANY)
SMEM = pl.BlockSpec(memory_space=pltpu.SMEM)
INSIDE = pl.BlockSpec(memory_space=pltpu.VMEM)
VMEM_LIMIT = 48 * 1024 * 1024


def sds(shape, dtype):
    return jax.ShapeDtypeStruct(tuple(shape), dtype)


def page_sizes(weights):
    depth1, gains1, inner1, outer1, depth2, gains2, inner2, outer2, down, up = weights
    return gains1.shape[-1], gains2.shape[-1], inner1.shape[-1], inner2.shape[-1]


def forward_call(where, fields, recv, weights, kept, stacks):
    c1, c2, e1, e2 = page_sizes(weights)
    last1, last2, stem = fields
    temps = [
        sds(recv.shape, F32), sds((3, 64, c2), F32), sds((3, 4, 64, c1), F32),
        sds((64, LANES), F32), sds((4, 64, LANES), F32), sds((64, e2), BF16), sds((256, e1), BF16),
    ]
    out_shape = temps + list(kept)
    wspecs = [INSIDE, INSIDE, ANY, ANY, INSIDE, INSIDE, ANY, ANY, ANY, ANY]
    in_specs = [SMEM] + [ANY] * 4 + wspecs + [ANY] * len(stacks)
    first_stack = 5 + len(weights)
    scratch = [
        pltpu.VMEM((4, 64, c1), F32), pltpu.VMEM((64, c2), F32), pltpu.VMEM((4, 64, c1), BF16),
        pltpu.VMEM((c1, e1), BF16), pltpu.VMEM((e1, c1), BF16),
        pltpu.VMEM((c2, e2), BF16), pltpu.VMEM((e2, c2), BF16),
        pltpu.VMEM((4 * c1, c2), BF16), pltpu.VMEM((c2, c1), BF16),
        pltpu.VMEM((4, 4, 64, c1), F32), pltpu.VMEM((7, 64, c2), F32),
        pltpu.VMEM((3, 64, c2), F32), pltpu.VMEM((3, 4, 64, c1), F32),
        pltpu.VMEM((64, LANES), F32), pltpu.VMEM((4, 64, LANES), F32),
        pltpu.VMEM((64, e2), BF16), pltpu.VMEM((256, e1), BF16),
    ]
    scratch += [pltpu.VMEM(s.shape[1:], s.dtype) for s in kept]
    scratch += [pltpu.VMEM((4, 64, c1), F32), pltpu.VMEM((64, c2), F32)]
    scratch += [pltpu.SemaphoreType.DMA((40,))]
    macs = 64 * (4 * c1 * c2 + 2 * c2 * e2 + c2 * c1) + 256 * 2 * c1 * e1
    outs = pl.pallas_call(
        forward_kernel,
        out_shape=out_shape,
        in_specs=in_specs,
        out_specs=[ANY] * len(out_shape),
        scratch_shapes=scratch,
        input_output_aliases={first_stack + k: len(temps) + k for k in range(len(stacks))},
        compiler_params=pltpu.CompilerParams(vmem_limit_bytes=VMEM_LIMIT),
        cost_estimate=pl.CostEstimate(flops=2 * macs, bytes_accessed=20 << 20, transcendentals=0),
        name="forward_page",
    )(where, last1, last2, stem, recv, *weights, *stacks)
    return outs[0], outs[1 : len(temps)], tuple(outs[len(temps) :])


def backward_call(where, fields, recv, prev, temps, weights, kept, stacks):
    c1, c2, e1, e2 = page_sizes(weights)
    last1, last2, teach1, teach2 = fields
    out_shape = [sds(recv.shape, F32)] + list(kept)
    wspecs = [INSIDE, INSIDE, ANY, ANY, INSIDE, INSIDE, ANY, ANY, ANY, ANY]
    lead = 1 + 4 + 2 + len(temps)
    in_specs = [SMEM] + [ANY] * (lead - 1) + wspecs + [ANY] * len(stacks)
    first_stack = lead + len(weights)
    scratch = [
        pltpu.VMEM((4, 64, c1), F32), pltpu.VMEM((64, c2), F32),
        pltpu.VMEM((4, 64, c1), BF16), pltpu.VMEM((64, c2), BF16),
        pltpu.VMEM((4, 64, c1), F32), pltpu.VMEM((64, c2), F32),
    ]
    scratch += [pltpu.VMEM(t.shape, t.dtype) for t in temps]
    scratch += [
        pltpu.VMEM((c1, e1), BF16), pltpu.VMEM((e1, c1), BF16),
        pltpu.VMEM((c2, e2), BF16), pltpu.VMEM((e2, c2), BF16),
        pltpu.VMEM((4 * c1, c2), BF16), pltpu.VMEM((c2, c1), BF16),
        pltpu.VMEM((4, 4, 64, c1), F32), pltpu.VMEM((7, 64, c2), F32),
        pltpu.VMEM((64, c2), F32), pltpu.VMEM((4, 64, c1), F32),
    ]
    held = [pltpu.VMEM(s.shape[1:], s.dtype) for s in kept]
    scratch += held[:6] + held[7:]
    scratch += [pltpu.VMEM((4, 64, c1), F32), pltpu.VMEM((64, c2), F32)]
    scratch += [pltpu.SemaphoreType.DMA((48,))]
    macs = 64 * (4 * c1 * c2 + 2 * c2 * e2 + c2 * c1) + 256 * 2 * c1 * e1
    outs = pl.pallas_call(
        backward_kernel,
        out_shape=out_shape,
        in_specs=in_specs,
        out_specs=[ANY] * len(out_shape),
        scratch_shapes=scratch,
        input_output_aliases={first_stack + k: 1 + k for k in range(len(stacks))},
        compiler_params=pltpu.CompilerParams(vmem_limit_bytes=VMEM_LIMIT),
        cost_estimate=pl.CostEstimate(flops=2 * macs, bytes_accessed=20 << 20, transcendentals=0),
        name="backward_page",
    )(where, last1, last2, teach1, teach2, recv, prev, *temps, *weights, *stacks)
    return outs[0], tuple(outs[1:])


def to_phases(field):
    pages, side, _, channels = field.shape
    half = side // 2
    shaped = field.reshape(pages, half, 2, half, 2, channels)
    return shaped.transpose(0, 2, 4, 1, 3, 5).reshape(pages, 4, half * half, channels)


def from_phases(field, side):
    pages, _, cells, channels = field.shape
    half = side // 2
    shaped = field.reshape(pages, 2, 2, half, half, channels)
    return shaped.transpose(0, 3, 1, 4, 2, 5).reshape(pages, side, side, channels)


def kept_shapes(pages, c1, c2, e1, e2):
    n = pages + 1
    ahead = (
        sds((n, 4, 64, c1), BF16), sds((n, 64, c2), BF16), sds((n, 64, e2), BF16),
        sds((n, 64, c2), BF16), sds((n, 256, c1), BF16), sds((n, 256, e1), BF16),
    )
    back = (
        sds((n, 64, c2), BF16), sds((n, 64, e2), BF16), sds((n, 64, c2), BF16),
        sds((n, 256, c1), BF16), sds((n, 256, e1), BF16), sds((n, 64, c1), BF16),
        sds((n, 4, 64, c1), F32), sds((n, 128, c2), F32),
    )
    return ahead, back


def plan(c1, c2, e1, e2, pieces):
    whole = (e2 // 2, c2 * e2 // (2 * c2), 2 * c1, c1 * e1 // (2 * c2), c1 * e1 // (2 * c2), c1 // 2)
    rows = [n // pieces for n in whole] + [8]
    starts = [sum(rows[:k]) for k in range(len(rows) + 1)]
    return rows, starts


def piece_index(bits, masks_count, group, rel):
    index = jnp.int32(group)
    for s in range(masks_count):
        own = bits[s if group == 0 else masks_count - 1 - s]
        index = 2 * index + (own + rel[s]) % 2
    return index


def rel_bits(value, count):
    return tuple((value >> (count - 1 - s)) & 1 for s in range(count))


def weight_kernel(levels, pages, sizes, where, *refs):
    c1, c2, e1, e2 = sizes
    pieces = 2 << levels
    rows, starts = plan(c1, c2, e1, e2, pieces)
    (
        patch, nrm2, act2, coarse, nrm1, act1, gout2, gpre2, glow, gout1, gpre1, gpool, small,
        first, later,
        v_patch, v_nrm2, v_act2, v_coarse, v_nrm1, v_act1,
        v_gout2, v_gpre2, v_glow, v_gout1, v_gpre1, v_gpool, v_small, flat, sems,
    ) = refs
    mv = Moves(sems)
    half = where[0]
    bits = [where[1 + s] for s in range(levels)]

    def part(ref, width):
        return ref.at[0:pages, :, pl.ds(pl.multiple_of(half * width, width), width)]

    w_act1 = mv.bring(part(act1, e1 // 2), v_act1)
    w_gout1 = mv.bring(gout1.at[0:pages], v_gout1)
    w_nrm1 = mv.bring(nrm1.at[0:pages], v_nrm1)
    w_gpre1 = mv.bring(part(gpre1, e1 // 2), v_gpre1)
    w_act2 = mv.bring(part(act2, e2 // 2), v_act2)
    w_gout2 = mv.bring(gout2.at[0:pages], v_gout2)
    w_nrm2 = mv.bring(nrm2.at[0:pages], v_nrm2)
    w_gpre2 = mv.bring(part(gpre2, e2 // 2), v_gpre2)
    w_patch = mv.bring(patch.at[0:pages, pl.ds(2 * half, 2)], v_patch)
    w_glow = mv.bring(glow.at[0:pages], v_glow)
    w_coarse = mv.bring(part(coarse, c2 // 2), v_coarse)
    w_gpool = mv.bring(gpool.at[0:pages], v_gpool)
    w_small = mv.bring(small.at[0:pages, pl.ds(pl.multiple_of(64 * half, 64), 64)], v_small)

    def flatten(value):
        return value.reshape(-1, value.shape[-1])

    def product(left, right):
        return lax.dot_general(left, right, (((0,), (0,)), ((), ())), preferred_element_type=F32)

    def place(section, row, value, lane=0):
        size = rows[section]
        done = 0
        while done < value.shape[0]:
            p, inside = divmod(row + done, size)
            count = min(size - inside, value.shape[0] - done)
            at = starts[section] + inside
            flat[p, at : at + count, lane : lane + value.shape[1]] = value[done : done + count]
            done += count

    w_act1.wait()
    w_gout1.wait()
    right = flatten(v_gout1[...])
    lanes = c2 // c1
    run = e1 // 2 // lanes
    for k in range(lanes):
        place(4, 0, product(flatten(v_act1[:, :, run * k : run * k + run]), right), c1 * k)
    w_nrm1.wait()
    w_gpre1.wait()
    left = flatten(v_nrm1[...])
    for k in range(e1 // 2 // c2):
        place(3, c1 * k, product(left, flatten(v_gpre1[:, :, c2 * k : c2 * k + c2])))
    w_act2.wait()
    w_gout2.wait()
    right = flatten(v_gout2[...])
    for r in range(0, e2 // 2, 256):
        place(0, r, product(flatten(v_act2[:, :, r : r + 256]), right))
    w_nrm2.wait()
    w_gpre2.wait()
    for k in range(e2 // 2 // c2):
        right = flatten(v_gpre2[:, :, c2 * k : c2 * k + c2])
        for r in range(0, c2, 256):
            place(1, c2 * k + r, product(flatten(v_nrm2[:, :, r : r + 256]), right))
    w_patch.wait()
    w_glow.wait()
    right = flatten(v_glow[...])
    for q in range(2):
        place(2, c1 * q, product(flatten(v_patch[:, q]), right))
    w_coarse.wait()
    w_gpool.wait()
    right = flatten(v_gpool[...])
    run = c2 // 2 // lanes
    for k in range(lanes):
        place(5, 0, product(flatten(v_coarse[:, :, run * k : run * k + run]), right), c1 * k)
    w_small.wait()
    total = v_small[0]
    for p in range(1, pages):
        total = total + v_small[p]
    for p in range(min(pieces, total.shape[0] // 8)):
        flat[p, starts[6] : starts[7], :] = total[8 * p : 8 * p + 8]
    for p in range(total.shape[0] // 8, pieces):
        flat[p, starts[6] : starts[7], :] = jnp.zeros((8, c2), F32)
    slot = 0
    each = pieces // 4
    for group in range(2):
        for value in range(2 * each):
            rel = rel_bits(value, levels)
            index = piece_index(bits, levels, group, rel)
            out = first if rel[0] == 1 else later
            mv.send(flat.at[index], out.at[each * group + value % each])
    mv.finish()


def weight_call(where, levels, pages, sizes, arrays):
    c1, c2, e1, e2 = sizes
    pieces = 2 << levels
    rows, starts = plan(c1, c2, e1, e2, pieces)
    scratch = [
        pltpu.VMEM((pages, 2, 64, c1), BF16), pltpu.VMEM((pages, 64, c2), BF16),
        pltpu.VMEM((pages, 64, e2 // 2), BF16), pltpu.VMEM((pages, 64, c2 // 2), BF16),
        pltpu.VMEM((pages, 256, c1), BF16), pltpu.VMEM((pages, 256, e1 // 2), BF16),
        pltpu.VMEM((pages, 64, c2), BF16), pltpu.VMEM((pages, 64, e2 // 2), BF16),
        pltpu.VMEM((pages, 64, c2), BF16), pltpu.VMEM((pages, 256, c1), BF16),
        pltpu.VMEM((pages, 256, e1 // 2), BF16), pltpu.VMEM((pages, 64, c1), BF16),
        pltpu.VMEM((pages, 64, c2), F32), pltpu.VMEM((pieces, starts[7], c2), F32),
        pltpu.SemaphoreType.DMA((16 + pieces,)),
    ]
    out = sds((pieces // 2, starts[7], c2), F32)
    macs = pages * (64 * (c1 * 4 * c2 + 2 * c2 * e2 + c2 * c1) + 256 * 2 * c1 * e1) // 2

    def kernel(*refs):
        weight_kernel(levels, pages, sizes, *refs)

    return pl.pallas_call(
        kernel,
        out_shape=[out, out],
        in_specs=[SMEM] + [ANY] * len(arrays),
        out_specs=[ANY, ANY],
        scratch_shapes=scratch,
        compiler_params=pltpu.CompilerParams(vmem_limit_bytes=VMEM_LIMIT),
        cost_estimate=pl.CostEstimate(flops=2 * macs, bytes_accessed=14 << 20, transcendentals=0),
        name="weight_half",
    )(where, *arrays)


def spread_kernel(levels, sizes, keys, where, *refs):
    c1, c2, e1, e2 = sizes
    pieces = 2 << levels
    rows, starts = plan(c1, c2, e1, e2, pieces)
    n = len(keys)
    parts = refs[:n]
    in1, out1, in2, out2, down, up, k1, s1, k2, s2, sems, done = refs[-12:]
    tail = done
    bits = [where[1 + s] for s in range(levels)]
    lanes = c2 // c1
    waits = []
    for k, (core, group, rel) in enumerate(keys):
        half = (where[0] + core) % 2
        p = piece_index(bits, levels, group, rel)
        src, sem = parts[k], sems.at[k]

        def go(section, dst, lane=None, src=src, sem=sem):
            piece = src.at[starts[section] : starts[section + 1]]
            if lane is not None:
                piece = piece.at[:, c1 * lane : c1 * lane + c1]
            pltpu.make_async_copy(piece, dst, sem).start()

        def span(base, count):
            return pl.ds(pl.multiple_of(base, count), count)

        go(0, out2.at[span(half * (e2 // 2) + rows[0] * p, rows[0]), :])
        per = c2 // rows[1]
        go(1, in2.at[
            span((p % per) * rows[1], rows[1]),
            span(half * (e2 // 2) + c2 * (p // per), c2),
        ])
        go(2, down.at[span(half * (2 * c1) + rows[2] * p, rows[2]), :])
        go(3, in1.at[span(rows[3] * p, rows[3]), span(half * (e1 // 2), c2)])
        for k2_ in range(lanes):
            run = e1 // 2 // lanes
            go(4, out1.at[span(half * (e1 // 2) + run * k2_ + rows[4] * p, rows[4]), :], k2_)
            run = c2 // 2 // lanes
            go(5, up.at[span(half * (c2 // 2) + run * k2_ + rows[5] * p, rows[5]), :], k2_)
        go(6, tail.at[span(pieces * 8 * half + 8 * p, 8), :])
        waits.append(pltpu.make_async_copy(src, src, sem))
    for copy in waits:
        copy.wait()
    base = [0, pieces * 8]
    k2[...] = tail[0:49, :]
    s2[...] = tail[56:64, :]
    k1[...] = tail[base[1] : base[1] + 49, 0:c1]
    s1[...] = tail[base[1] + 56 : base[1] + 64, 0:c1]


def spread_call(where, levels, sizes, table):
    c1, c2, e1, e2 = sizes
    pieces = 2 << levels
    keys = sorted(table)
    parts = [table[k] for k in keys]
    outs = [
        sds((c1, e1), F32), sds((e1, c1), F32), sds((c2, e2), F32), sds((e2, c2), F32),
        sds((4 * c1, c2), F32), sds((c2, c1), F32),
        sds((49, c1), F32), sds((8, c1), F32), sds((49, c2), F32), sds((8, c2), F32),
    ]

    def kernel(*refs):
        spread_kernel(levels, sizes, keys, *refs)

    return pl.pallas_call(
        kernel,
        out_shape=outs,
        in_specs=[SMEM] + [ANY] * len(parts),
        out_specs=[ANY] * 6 + [INSIDE] * 4,
        scratch_shapes=[pltpu.SemaphoreType.DMA((len(parts),)), pltpu.VMEM((16 * pieces, c2), F32)],
        compiler_params=pltpu.CompilerParams(vmem_limit_bytes=VMEM_LIMIT),
        cost_estimate=pl.CostEstimate(flops=0, bytes_accessed=26 << 20, transcendentals=0),
        name="spread",
    )(where, *parts)


def swap(value, mask):
    return lax.ppermute(value, "dp", [(i, i ^ mask) for i in range(lax.axis_size("dp"))])


def sum_weights(arrays, pages, sizes):
    devices = lax.axis_size("dp")
    levels = devices.bit_length() - 2
    index = lax.axis_index("dp")
    masks = [2 << s for s in range(levels)]
    order = [masks, masks[::-1]]
    core = index % 2
    bits = [(index // m) % 2 for m in masks]
    where = jnp.stack([core] + bits).astype(jnp.int32)
    other = jnp.stack([1 - core] + bits).astype(jnp.int32)
    their_first, their_later = weight_call(other, levels, pages, sizes, arrays)
    got_first = swap(their_first, 1)
    my_first, my_later = weight_call(where, levels, pages, sizes, arrays)
    got_later = swap(their_later, 1)
    each = 1 << (levels - 1)
    held = {}
    for group in range(2):
        for value in range(2 * each):
            rel = rel_bits(value, levels)
            mine, got = (my_first, got_first) if rel[0] else (my_later, got_later)
            k = each * group + value % each
            held[group, rel] = mine[k] + got[k]
    for s in range(levels):
        for value in reversed(range(1 << (levels - 1 - s))):
            for group in range(2):
                rest = rel_bits(value, levels - 1 - s)
                there, here = (0,) * s + (1,) + rest, (0,) * (s + 1) + rest
                arrived = swap(held.pop((group, there)), order[group][s])
                held[group, here] = held[group, here] + arrived
    table = {}

    def keep(group, rel, value):
        table[0, group, rel] = value
        table[1, group, rel] = swap(value, 1)

    for group in range(2):
        keep(group, (0,) * levels, held[group, (0,) * levels])
    for s in reversed(range(levels)):
        for value in range(1 << (levels - 1 - s)):
            for group in range(2):
                rest = rel_bits(value, levels - 1 - s)
                here, there = (0,) * (s + 1) + rest, (0,) * s + (1,) + rest
                keep(group, there, swap(table[0, group, here], order[group][s]))
    return spread_call(where, levels, sizes, table)


def local(
    stem_map, last_one, last_two, teach_one, teach_two, teacher_slot,
    depth_one, gains_one, inner_one, outer_one, depth_two, gains_two, inner_two, outer_two,
    down_proj, up_proj,
):
    columns = lax.axis_size("col")
    position = lax.axis_index("col")
    pages, side = stem_map.shape[0], stem_map.shape[1]
    c1, c2 = last_one.shape[-1], last_two.shape[-1]
    sizes = (c1, c2, inner_one.shape[-1], inner_two.shape[-1])
    last1 = to_phases(last_one)
    last2 = last_two.reshape(pages, 64, c2)
    stem = to_phases(stem_map)
    teach1 = to_phases(teach_one)
    teach2 = teach_two.reshape(pages, 64, c2)
    weights = (
        depth_one[0].astype(F32), gains_one[0], inner_one[0], outer_one[0],
        depth_two[0].astype(F32), gains_two[0], inner_two[0], outer_two[0],
        down_proj[0], up_proj[0],
    )
    first = (position == columns - 1).astype(jnp.int32)
    route = [(i, i - 1) for i in range(1, columns)]
    ahead_shapes, back_shapes = kept_shapes(pages, *sizes)
    blank = jnp.zeros((6, 64, c1), F32)

    def slot(k, out_grad, recv_high, ahead, back):
        micro = k - (columns - 1 - position)
        active = jnp.logical_and(micro >= 0, micro < pages)
        page = jnp.clip(micro, 0, pages - 1)
        spot = jnp.where(active, micro, pages)
        where = jnp.stack([page, spot, first, teacher_slot[page]]).astype(jnp.int32)
        recv_grad = blank if out_grad is None else lax.ppermute(out_grad, "col", route)
        prev, temps, ahead = forward_call(
            where, (last1, last2, stem), recv_high, weights, ahead_shapes, ahead
        )
        next_high = lax.ppermute(prev, "col", route)
        out_grad, back = backward_call(
            where, (last1, last2, teach1, teach2), recv_grad, prev, temps, weights,
            back_shapes, back,
        )
        return out_grad, next_high, ahead, back

    begun = slot(jnp.int32(0), None, blank, (), ())
    _, _, ahead, back = lax.fori_loop(
        1, columns + pages - 1, lambda k, carried: slot(k, *carried), begun
    )
    stem_total = from_phases(lax.psum(back[6][:pages], "col"), side)
    in1, out1, in2, out2, down, up, k1, s1, k2, s2 = sum_weights(
        ahead + back[:6] + back[7:], pages, sizes
    )
    return (
        k1[None], s1[None, :3], in1[None], out1[None], k2[None], s2[None, :2], s2[2:3],
        in2[None], out2[None], down[None], up[None], stem_total,
    )


def solution(mesh):
    paged, row, mat = P("dp", None, None, None), P("col", None), P("col", None, None)
    return jax.shard_map(
        local,
        mesh=mesh,
        in_specs=(paged,) * 5 + (P("dp"),) + (mat,) * 10,
        out_specs=(mat,) * 6 + (row,) + (mat,) * 4 + (paged,),
        check_vma=False,
    )
```

time: 1100 us -> 716 us (0.65)
  Pallas kernels: 0 us -> 480 us
  other arithmetic: 315 us -> 15.7 us
  waiting for transfers between devices: 376 us -> 126 us
  matrix products: 163 us -> 0 us
  local copies, waits for them, and re-layouts: 135 us -> 34.6 us
  blocking collectives: 24.1 us -> 0 us
  loops' own time: 21 us -> 1.2 us
    pallas_call x0 -> x21, Pallas kernels: none -> 480 us  [the longest x1 300 us: spread_call(): pl.pallas_call(kernel, out_shape=outs, in_specs=[SMEM] + [ANY] * len(part...]
    psum x2 -> x1, waiting for transfers between devices: 233 us -> 0.01 us  [local(): stem_total = from_phases(lax.psum(back[6][:pages], 'col'), side)]
    dot_general x108 -> x0, matrix products: 163 us -> none  [the longest x36 76.4 us: contract(): lax.dot_general(left_flat, right_flat, (((0,), (0,)), ((), ())), preferre...]
    add x96 -> x4, other arithmetic: 167 us -> 7.94 us  [the longest x3 5.07 us: sum_weights(): held[group, here] = held[group, here] + arrived]
    reduce_sum x78 -> x0, other arithmetic: 47.2 us -> none  [the longest x12 24.7 us: norm_part(): center = hidden - jnp.mean(hidden, axis=-1, keepdims=True)]
    slice x37 -> x2, local copies, waits for them, and re-layouts: 38.4 us -> 0.68 us  [the longest x1 0.58 us: local(): s2[2:3]]
    add_any x30 -> x0, other arithmetic: 34.6 us -> none  [the longest x18 24.1 us: depthwise(): padded[:, row_offset:row_offset + side_cells, col_offset:col_offset + sid...]
    mul x42 -> x0, other arithmetic: 33.3 us -> none  [the longest x36 28.9 us: depthwise(): padded[:, row_offset:row_offset + side_cells, col_offset:col_offset + sid...]
  transfers between devices with their start and end apart: 38 -> 40, of which waited for: 14 -> 30; matrix products, arithmetic and copies ran while one was open for 16% -> 5% of each run, Pallas kernels for 0% -> 65%
where the time goes in v1:
time: 716 us; the launch traced here: 712 us
  Pallas kernels  480 us (67%)
  waiting for transfers between devices  126 us (18%)
  starting transfers between devices  39.7 us (6%)
  local copies, waits for them, and re-layouts  34.6 us (5%)
  other arithmetic  15.7 us (2%)
  between operations  14.5 us (2%)
    pallas_call x1, Pallas kernels, spread_call(): pl.pallas_call(kernel, out_shape=outs, in_specs=[SMEM] + [ANY] * len(part...  300 us
    ppermute x22, waiting for transfers between devices, swap(): lax.ppermute(value, 'dp', [(i, i ^ mask) for i in range(lax.axis_size('dp...  95.1 us
    pallas_call x9, Pallas kernels, backward_call(): pl.pallas_call(backward_kernel, out_shape=out_shape, in_specs=in_specs, o...  86.1 us
    pallas_call x9, Pallas kernels, forward_call(): pl.pallas_call(forward_kernel, out_shape=out_shape, in_specs=in_specs, ou...  79.2 us
    ppermute x9, waiting for transfers between devices, slot(): next_high = lax.ppermute(prev, 'col', route)  25.9 us
    ppermute x22, starting transfers between devices, swap(): lax.ppermute(value, 'dp', [(i, i ^ mask) for i in range(lax.axis_size('dp...  17.8 us
    pallas_call x2, Pallas kernels, weight_call(): pl.pallas_call(kernel, out_shape=[out, out], in_specs=[SMEM] + [ANY] * le...  15.2 us
  transfers between devices with their start and end apart: 40, of which 30 were waited for; matrix products, arithmetic and copies ran while one was open for 5% of the time, Pallas kernels for 65%

profile of v1, /device:TPU:0, one launch (start us, length us, event | category | flops | bytes accessed | tf_op | source)
XLA Modules:
  0.0 711.5 jit_solution(10964798933459948063)
XLA Ops:
  7.2 2.2 reshape.66
  15.6 8.0 %forward_page.8 = (f32[6,64,256]{2,1,0:T(8,128)S(1)}, f32[3,64,512]{2,1,0:T(8,128)S(1)}, f32[3,4,64,256]{3,2,1,0:T(8,128)S(1)}, f32[64,128]{1,0:T(8,128)S(1)}, f...) custom-call(s32[4]{0:T(128)S(1)} %pad_add_fusion.1.where, ...), custom_call_target="tpu_custom_call" | custom-call | flops 620756992 | bytes 20971520 | tf_op jit(solution)/shard_map/forward_page/pallas_call | solution.py:482
  24.9 2.9 reshape.69
  27.8 2.2 copy.43
  29.9 10.3 %backward_page.8 = (f32[6,64,256]{2,1,0:T(8,128)}, bf16[7,64,512]{2,1,0:T(8,128)(2,1)}, bf16[7,64,2048]{2,1,0:T(8,128)(2,1)}, bf16[7,64,512]{2,1,0:T(8,128)(2,1)...) custom-call(s32[4]{0:T(128)S(1)} %pad_add_fusion.1.where, ...), custom_call_target="tpu_custom_call" | custom-call | flops 620756992 | bytes 20971520 | tf_op jit(solution)/shard_map/backward_page/pallas_call | solution.py:522
  40.3 215.7 %while.45 = (s32[]{:T(128)}, f32[6,64,256]{2,1,0:T(8,128)}, f32[6,64,256]{2,1,0:T(8,128)}, bf16[7,4,64,256]{3,2,1,0:T(8,128)(2,1)}, bf16[7,64,512]{2,1,0:T(8,128...) while((s32[]{:T(128)}, f32[6,64,256]{2,1,0:T(8,128)}, ...), condition=%wide.region_1.2_spmd, body=%wide.region_0.1_spmd.sunk | while | flops 1241513984 | bytes 119939880 | solution.py:883
  43.7 8.9 %forward_page.9 = (f32[6,64,256]{2,1,0:T(8,128)S(1)}, f32[3,64,512]{2,1,0:T(8,128)S(1)}, f32[3,4,64,256]{3,2,1,0:T(8,128)S(1)}, f32[64,128]{1,0:T(8,128)S(1)}, f...) custom-call(s32[4]{0:T(128)S(1)} %pad_add_fusion.3.where, ...), custom_call_target="tpu_custom_call", output_to_operand_aliasing={{7}: (15, {}), {8}: (16, {}), {9}: (17, {}), {10}: (18, {})... | custom-call | flops 620756992 | bytes 20971520 | tf_op jit(solution)/shard_map/while/body/eval_jaxpr/forward_page/pallas_call | solution.py:482
  55.2 9.5 %backward_page.9 = (f32[6,64,256]{2,1,0:T(8,128)}, bf16[7,64,512]{2,1,0:T(8,128)(2,1)}, bf16[7,64,2048]{2,1,0:T(8,128)(2,1)S(1)}, bf16[7,64,512]{2,1,0:T(8,128)(...) custom-call(s32[4]{0:T(128)S(1)} %pad_add_fusion.3.where, ...), custom_call_target="tpu_custom_call", output_to_operand_aliasing={{1}: (23, {}), {2}: (24, {}), {3}: (25, {}), {4}: (26, {}),... | custom-call | flops 620756992 | bytes 20971520 | tf_op jit(solution)/shard_map/while/body/eval_jaxpr/backward_page/pallas_call | solution.py:522
  64.7 3.2 collective-permute-done.1
  71.3 8.9 %forward_page.9 = (f32[6,64,256]{2,1,0:T(8,128)S(1)}, f32[3,64,512]{2,1,0:T(8,128)S(1)}, f32[3,4,64,256]{3,2,1,0:T(8,128)S(1)}, f32[64,128]{1,0:T(8,128)S(1)}, f...) custom-call(s32[4]{0:T(128)S(1)} %pad_add_fusion.3.where, ...), custom_call_target="tpu_custom_call", output_to_operand_aliasing={{7}: (15, {}), {8}: (16, {}), {9}: (17, {}), {10}: (18, {})... | custom-call | flops 620756992 | bytes 20971520 | tf_op jit(solution)/shard_map/while/body/eval_jaxpr/forward_page/pallas_call | solution.py:482
  82.1 9.5 %backward_page.9 = (f32[6,64,256]{2,1,0:T(8,128)}, bf16[7,64,512]{2,1,0:T(8,128)(2,1)}, bf16[7,64,2048]{2,1,0:T(8,128)(2,1)S(1)}, bf16[7,64,512]{2,1,0:T(8,128)(...) custom-call(s32[4]{0:T(128)S(1)} %pad_add_fusion.3.where, ...), custom_call_target="tpu_custom_call", output_to_operand_aliasing={{1}: (23, {}), {2}: (24, {}), {3}: (25, {}), {4}: (26, {}),... | custom-call | flops 620756992 | bytes 20971520 | tf_op jit(solution)/shard_map/while/body/eval_jaxpr/backward_page/pallas_call | solution.py:522
  91.6 3.2 collective-permute-done.1
  98.2 8.9 %forward_page.9 = (f32[6,64,256]{2,1,0:T(8,128)S(1)}, f32[3,64,512]{2,1,0:T(8,128)S(1)}, f32[3,4,64,256]{3,2,1,0:T(8,128)S(1)}, f32[64,128]{1,0:T(8,128)S(1)}, f...) custom-call(s32[4]{0:T(128)S(1)} %pad_add_fusion.3.where, ...), custom_call_target="tpu_custom_call", output_to_operand_aliasing={{7}: (15, {}), {8}: (16, {}), {9}: (17, {}), {10}: (18, {})... | custom-call | flops 620756992 | bytes 20971520 | tf_op jit(solution)/shard_map/while/body/eval_jaxpr/forward_page/pallas_call | solution.py:482
  109.0 9.5 %backward_page.9 = (f32[6,64,256]{2,1,0:T(8,128)}, bf16[7,64,512]{2,1,0:T(8,128)(2,1)}, bf16[7,64,2048]{2,1,0:T(8,128)(2,1)S(1)}, bf16[7,64,512]{2,1,0:T(8,128)(...) custom-call(s32[4]{0:T(128)S(1)} %pad_add_fusion.3.where, ...), custom_call_target="tpu_custom_call", output_to_operand_aliasing={{1}: (23, {}), {2}: (24, {}), {3}: (25, {}), {4}: (26, {}),... | custom-call | flops 620756992 | bytes 20971520 | tf_op jit(solution)/shard_map/while/body/eval_jaxpr/backward_page/pallas_call | solution.py:522
  118.5 3.2 collective-permute-done.1
  125.1 8.9 %forward_page.9 = (f32[6,64,256]{2,1,0:T(8,128)S(1)}, f32[3,64,512]{2,1,0:T(8,128)S(1)}, f32[3,4,64,256]{3,2,1,0:T(8,128)S(1)}, f32[64,128]{1,0:T(8,128)S(1)}, f...) custom-call(s32[4]{0:T(128)S(1)} %pad_add_fusion.3.where, ...), custom_call_target="tpu_custom_call", output_to_operand_aliasing={{7}: (15, {}), {8}: (16, {}), {9}: (17, {}), {10}: (18, {})... | custom-call | flops 620756992 | bytes 20971520 | tf_op jit(solution)/shard_map/while/body/eval_jaxpr/forward_page/pallas_call | solution.py:482
  135.8 9.5 %backward_page.9 = (f32[6,64,256]{2,1,0:T(8,128)}, bf16[7,64,512]{2,1,0:T(8,128)(2,1)}, bf16[7,64,2048]{2,1,0:T(8,128)(2,1)S(1)}, bf16[7,64,512]{2,1,0:T(8,128)(...) custom-call(s32[4]{0:T(128)S(1)} %pad_add_fusion.3.where, ...), custom_call_target="tpu_custom_call", output_to_operand_aliasing={{1}: (23, {}), {2}: (24, {}), {3}: (25, {}), {4}: (26, {}),... | custom-call | flops 620756992 | bytes 20971520 | tf_op jit(solution)/shard_map/while/body/eval_jaxpr/backward_page/pallas_call | solution.py:522
  145.3 3.2 collective-permute-done.1
  151.9 8.9 %forward_page.9 = (f32[6,64,256]{2,1,0:T(8,128)S(1)}, f32[3,64,512]{2,1,0:T(8,128)S(1)}, f32[3,4,64,256]{3,2,1,0:T(8,128)S(1)}, f32[64,128]{1,0:T(8,128)S(1)}, f...) custom-call(s32[4]{0:T(128)S(1)} %pad_add_fusion.3.where, ...), custom_call_target="tpu_custom_call", output_to_operand_aliasing={{7}: (15, {}), {8}: (16, {}), {9}: (17, {}), {10}: (18, {})... | custom-call | flops 620756992 | bytes 20971520 | tf_op jit(solution)/shard_map/while/body/eval_jaxpr/forward_page/pallas_call | solution.py:482
  162.7 9.5 %backward_page.9 = (f32[6,64,256]{2,1,0:T(8,128)}, bf16[7,64,512]{2,1,0:T(8,128)(2,1)}, bf16[7,64,2048]{2,1,0:T(8,128)(2,1)S(1)}, bf16[7,64,512]{2,1,0:T(8,128)(...) custom-call(s32[4]{0:T(128)S(1)} %pad_add_fusion.3.where, ...), custom_call_target="tpu_custom_call", output_to_operand_aliasing={{1}: (23, {}), {2}: (24, {}), {3}: (25, {}), {4}: (26, {}),... | custom-call | flops 620756992 | bytes 20971520 | tf_op jit(solution)/shard_map/while/body/eval_jaxpr/backward_page/pallas_call | solution.py:522
  172.2 3.2 collective-permute-done.1
  178.8 8.9 %forward_page.9 = (f32[6,64,256]{2,1,0:T(8,128)S(1)}, f32[3,64,512]{2,1,0:T(8,128)S(1)}, f32[3,4,64,256]{3,2,1,0:T(8,128)S(1)}, f32[64,128]{1,0:T(8,128)S(1)}, f...) custom-call(s32[4]{0:T(128)S(1)} %pad_add_fusion.3.where, ...), custom_call_target="tpu_custom_call", output_to_operand_aliasing={{7}: (15, {}), {8}: (16, {}), {9}: (17, {}), {10}: (18, {})... | custom-call | flops 620756992 | bytes 20971520 | tf_op jit(solution)/shard_map/while/body/eval_jaxpr/forward_page/pallas_call | solution.py:482
  189.6 9.5 %backward_page.9 = (f32[6,64,256]{2,1,0:T(8,128)}, bf16[7,64,512]{2,1,0:T(8,128)(2,1)}, bf16[7,64,2048]{2,1,0:T(8,128)(2,1)S(1)}, bf16[7,64,512]{2,1,0:T(8,128)(...) custom-call(s32[4]{0:T(128)S(1)} %pad_add_fusion.3.where, ...), custom_call_target="tpu_custom_call", output_to_operand_aliasing={{1}: (23, {}), {2}: (24, {}), {3}: (25, {}), {4}: (26, {}),... | custom-call | flops 620756992 | bytes 20971520 | tf_op jit(solution)/shard_map/while/body/eval_jaxpr/backward_page/pallas_call | solution.py:522
  199.1 3.2 collective-permute-done.1
  205.7 8.9 %forward_page.9 = (f32[6,64,256]{2,1,0:T(8,128)S(1)}, f32[3,64,512]{2,1,0:T(8,128)S(1)}, f32[3,4,64,256]{3,2,1,0:T(8,128)S(1)}, f32[64,128]{1,0:T(8,128)S(1)}, f...) custom-call(s32[4]{0:T(128)S(1)} %pad_add_fusion.3.where, ...), custom_call_target="tpu_custom_call", output_to_operand_aliasing={{7}: (15, {}), {8}: (16, {}), {9}: (17, {}), {10}: (18, {})... | custom-call | flops 620756992 | bytes 20971520 | tf_op jit(solution)/shard_map/while/body/eval_jaxpr/forward_page/pallas_call | solution.py:482
  216.4 9.5 %backward_page.9 = (f32[6,64,256]{2,1,0:T(8,128)}, bf16[7,64,512]{2,1,0:T(8,128)(2,1)}, bf16[7,64,2048]{2,1,0:T(8,128)(2,1)S(1)}, bf16[7,64,512]{2,1,0:T(8,128)(...) custom-call(s32[4]{0:T(128)S(1)} %pad_add_fusion.3.where, ...), custom_call_target="tpu_custom_call", output_to_operand_aliasing={{1}: (23, {}), {2}: (24, {}), {3}: (25, {}), {4}: (26, {}),... | custom-call | flops 620756992 | bytes 20971520 | tf_op jit(solution)/shard_map/while/body/eval_jaxpr/backward_page/pallas_call | solution.py:522
  225.9 3.2 collective-permute-done.1
  232.5 8.9 %forward_page.9 = (f32[6,64,256]{2,1,0:T(8,128)S(1)}, f32[3,64,512]{2,1,0:T(8,128)S(1)}, f32[3,4,64,256]{3,2,1,0:T(8,128)S(1)}, f32[64,128]{1,0:T(8,128)S(1)}, f...) custom-call(s32[4]{0:T(128)S(1)} %pad_add_fusion.3.where, ...), custom_call_target="tpu_custom_call", output_to_operand_aliasing={{7}: (15, {}), {8}: (16, {}), {9}: (17, {}), {10}: (18, {})... | custom-call | flops 620756992 | bytes 20971520 | tf_op jit(solution)/shard_map/while/body/eval_jaxpr/forward_page/pallas_call | solution.py:482
  243.3 9.5 %backward_page.9 = (f32[6,64,256]{2,1,0:T(8,128)}, bf16[7,64,512]{2,1,0:T(8,128)(2,1)}, bf16[7,64,2048]{2,1,0:T(8,128)(2,1)S(1)}, bf16[7,64,512]{2,1,0:T(8,128)(...) custom-call(s32[4]{0:T(128)S(1)} %pad_add_fusion.3.where, ...), custom_call_target="tpu_custom_call", output_to_operand_aliasing={{1}: (23, {}), {2}: (24, {}), {3}: (25, {}), {4}: (26, {}),... | custom-call | flops 620756992 | bytes 20971520 | tf_op jit(solution)/shard_map/while/body/eval_jaxpr/backward_page/pallas_call | solution.py:522
  252.8 3.2 collective-permute-done.1
  256.1 8.0 %weight_half.3 = (f32[4,408,512]{2,1,0:T(8,128)S(1)}, f32[4,408,512]{2,1,0:T(8,128)}) custom-call(s32[3]{0:T(128)S(1)} %add_add_fusion.1.refs_0_, bf16[7,4,64,256]{3,2,1,0:T(8,128)(2,1)} %get-tuple-element.848.refs_1_, bf16[7,64,512]{2,1,0:T(8,128)(2,1)} %get-tuple-element.849.refs_2_, bf16[7,64,2048]{2,1,0:T(8,128)(2,1)} %get-tuple-element.850.refs_3_, ...), custom_call_target="tpu_custom_call" | custom-call | flops 1862270976 | bytes 14680064 | tf_op jit(solution)/shard_map/weight_half/pallas_call | solution.py:703
  264.8 7.3 %weight_half.2 = (f32[4,408,512]{2,1,0:T(8,128)S(1)}, f32[4,408,512]{2,1,0:T(8,128)}) custom-call(s32[3]{0:T(128)S(1)} %add_add_fusion.refs_0_, bf16[7,4,64,256]{3,2,1,0:T(8,128)(2,1)S(1)} %copy-done.14, bf16[7,64,512]{2,1,0:T(8,128)(2,1)S(1)} %copy-done.16, bf16[7,64,2048]{2,1,0:T(8,128)(2,1)S(1)} %copy-done.8, ...), custom_call_target="tpu_custom_call" | custom-call | flops 1862270976 | bytes 14680064 | tf_op jit(solution)/shard_map/weight_half/pallas_call | solution.py:703
  272.1 2.1 collective-permute-done.4
  274.2 2.9 fusion.3
  280.8 17.8 %collective-permute-done.12 = f32[408,512]{1,0:T(8,128)S(1)} collective-permute-done((f32[408,512]{1,0:T(8,128)S(1)}, f32[408,512]{1,0:T(8,128)S(1)}, u32[]{:S(2)}, u32[]{:S(2)}) %collective-permute-start.12) | collective-permute-done | bytes 835616 | tf_op jit(solution)/shard_map/ppermute | solution.py:791
  302.1 13.6 %collective-permute-done.11 = f32[408,512]{1,0:T(8,128)S(1)} collective-permute-done((f32[408,512]{1,0:T(8,128)S(1)}, f32[408,512]{1,0:T(8,128)S(1)}, u32[]{:S(2)}, u32[]{:S(2)}) %collective-permute-start.11) | collective-permute-done | bytes 835616 | tf_op jit(solution)/shard_map/ppermute | solution.py:791
  315.7 5.9 collective-permute-done.13
  321.6 2.1 fusion.6
  327.5 12.0 %collective-permute-done.5 = f32[408,512]{1,0:T(8,128)S(1)} collective-permute-done((f32[408,512]{1,0:T(8,128)S(1)}, f32[408,512]{1,0:T(8,128)S(1)}, u32[]{:S(2)}, u32[]{:S(2)}) %collective-permute-start.5) | collective-permute-done | bytes 835616 | tf_op jit(solution)/shard_map/ppermute | solution.py:791
  339.5 5.8 collective-permute-done.7
  350.1 7.3 %collective-permute-done.14.refs_6_ = f32[408,512]{1,0:T(8,128)S(1)} collective-permute-done((f32[408,512]{1,0:T(8,128)S(1)}, f32[408,512]{1,0:T(8,128)S(1)}, u32[]{:S(2)}, u32[]{:S(2)}) %collective-permute-start.14) | collective-permute-done | bytes 835616 | tf_op jit(solution)/shard_map/ppermute | solution.py:791
  357.4 5.8 collective-permute-done.15.refs_7_
  364.9 16.3 %collective-permute-done.8.refs_2_ = f32[408,512]{1,0:T(8,128)} collective-permute-done((f32[408,512]{1,0:T(8,128)S(1)}, f32[408,512]{1,0:T(8,128)}, u32[]{:S(2)}, u32[]{:S(2)}) %collective-permute-start.8) | collective-permute-done | bytes 835616 | tf_op jit(solution)/shard_map/ppermute | solution.py:791
  383.0 2.4 copy.54
  385.4 3.1 reshape.75
  389.1 4.0 collective-permute-done.16.refs_8_
  399.1 299.7 %spread.1 = (f32[256,1024]{1,0:T(8,128)}, f32[1024,256]{1,0:T(8,128)}, f32[512,2048]{1,0:T(8,128)}, f32[2048,512]{1,0:T(8,128)}, f32[1024,512]{1,0:T(8,128)}, /*...) custom-call(s32[3]{0:T(128)S(1)} %add_add_fusion.refs_0_, ...), custom_call_target="tpu_custom_call" | custom-call | bytes 27262976 | tf_op jit(solution)/shard_map/spread/pallas_call | solution.py:778
  701.9 2.8 copy.123
  (302 shorter events, 78.6 us)
Async XLA Ops:
  7.2 694.7 %all-reduce.2.cloned.1.call-start = ((), (), s32[]{:S(2)}) async-start(), calls=%async_computation | async-start | bytes 3145728 | tf_op jit(solution)/shard_map/psum | solution.py:886
  23.6 16.7 %collective-permute-start.2 = (f32[6,64,256]{2,1,0:T(8,128)S(1)}, f32[6,64,256]{2,1,0:T(8,128)}, u32[]{:S(2)}, u32[]{:S(2)}) collective-permute-start(f32[6,64,256]{2,1,0:T(8,128)S(1)} %get-tuple-element.826.prev), channel_id=1, source_target_pairs={{8,0},{16,8},{24,16},{9,1},{17,9},{25,17},{10,2},{18,10},{26,18},{... | collective-permute-start | bytes 1179656 | tf_op jit(solution)/shard_map/ppermute | solution.py:875
  40.3 14.9 %collective-permute-start = (f32[6,64,256]{2,1,0:T(8,128)}, f32[6,64,256]{2,1,0:T(8,128)S(1)}, u32[]{:S(2)}, u32[]{:S(2)}) collective-permute-start(f32[6,64,256]{2,1,0:T(8,128)} %get-tuple-element.1259), channel_id=1, source_target_pairs={{8,0},{16,8},{24,16},{9,1},{17,9},{25,17},{10,2},{18,10},{26,18},{... | collective-permute-start | bytes 1179656 | tf_op jit(solution)/shard_map/while/body/eval_jaxpr/ppermute | solution.py:871
  43.6 11.6 %copy-start.4 = (bf16[7,256,1024]{2,1,0:T(8,128)(2,1)S(1)}, bf16[7,256,1024]{2,1,0:T(8,128)(2,1)}, u32[]{:S(2)}) copy-start(bf16[7,256,1024]{2,1,0:T(8,128)(2,1)} %get-tuple-element.1271.rest_4_) | copy-start | bytes 11010052 | tf_op jit(solution)/shard_map/while
  43.6 11.6 %copy-start.6 = (bf16[1024,512]{1,0:T(8,128)(2,1)S(1)}, bf16[1024,512]{1,0:T(8,128)(2,1)}, u32[]{:S(2)}) copy-start(bf16[1024,512]{1,0:T(8,128)(2,1)} %get-tuple-element.1328.down) | copy-start | bytes 3145732 | tf_op jit(solution)/shard_map/while
  43.6 11.6 %copy-start.7 = (f32[6,64,512]{2,1,0:T(8,128)S(1)}, f32[6,64,512]{2,1,0:T(8,128)}, u32[]{:S(2)}) copy-start(f32[6,64,512]{2,1,0:T(8,128)} %get-tuple-element.1318.last2) | copy-start | bytes 2359300 | tf_op jit(solution)/shard_map/while
  43.6 11.6 %copy-start.9 = (bf16[7,64,2048]{2,1,0:T(8,128)(2,1)S(1)}, bf16[7,64,2048]{2,1,0:T(8,128)(2,1)}, u32[]{:S(2)}) copy-start(bf16[7,64,2048]{2,1,0:T(8,128)(2,1)} %get-tuple-element.1268.rest_1_) | copy-start | bytes 5505028 | tf_op jit(solution)/shard_map/while
  43.6 11.6 %copy-start.17 = (f32[49,512]{1,0:T(8,128)S(1)}, f32[49,512]{1,0:T(8,128)}, u32[]{:S(2)}) copy-start(f32[49,512]{1,0:T(8,128)} %get-tuple-element.1324.depth2) | copy-start | bytes 301060 | tf_op jit(solution)/shard_map/while
  52.6 15.4 %collective-permute-start.1 = (f32[6,64,256]{2,1,0:T(8,128)S(1)}, f32[6,64,256]{2,1,0:T(8,128)}, u32[]{:S(2)}, u32[]{:S(2)}) collective-permute-start(f32[6,64,256]{2,1,0:T(8,128)S(1)} %get-tuple-element.1197.prev), channel_id=1, source_target_pairs={{8,0},{16,8},{24,16},{9,1},{17,9},{25,17},{10,2},{18,10},{26,18},{... | collective-permute-start | bytes 1179656 | tf_op jit(solution)/shard_map/while/body/eval_jaxpr/ppermute | solution.py:875
  68.0 14.0 %collective-permute-start = (f32[6,64,256]{2,1,0:T(8,128)}, f32[6,64,256]{2,1,0:T(8,128)S(1)}, u32[]{:S(2)}, u32[]{:S(2)}) collective-permute-start(f32[6,64,256]{2,1,0:T(8,128)} %get-tuple-element.1259), channel_id=1, source_target_pairs={{8,0},{16,8},{24,16},{9,1},{17,9},{25,17},{10,2},{18,10},{26,18},{... | collective-permute-start | bytes 1179656 | tf_op jit(solution)/shard_map/while/body/eval_jaxpr/ppermute | solution.py:871
  80.2 14.6 %collective-permute-start.1 = (f32[6,64,256]{2,1,0:T(8,128)S(1)}, f32[6,64,256]{2,1,0:T(8,128)}, u32[]{:S(2)}, u32[]{:S(2)}) collective-permute-start(f32[6,64,256]{2,1,0:T(8,128)S(1)} %get-tuple-element.1197.prev), channel_id=1, source_target_pairs={{8,0},{16,8},{24,16},{9,1},{17,9},{25,17},{10,2},{18,10},{26,18},{... | collective-permute-start | bytes 1179656 | tf_op jit(solution)/shard_map/while/body/eval_jaxpr/ppermute | solution.py:875
  94.8 14.1 %collective-permute-start = (f32[6,64,256]{2,1,0:T(8,128)}, f32[6,64,256]{2,1,0:T(8,128)S(1)}, u32[]{:S(2)}, u32[]{:S(2)}) collective-permute-start(f32[6,64,256]{2,1,0:T(8,128)} %get-tuple-element.1259), channel_id=1, source_target_pairs={{8,0},{16,8},{24,16},{9,1},{17,9},{25,17},{10,2},{18,10},{26,18},{... | collective-permute-start | bytes 1179656 | tf_op jit(solution)/shard_map/while/body/eval_jaxpr/ppermute | solution.py:871
  107.1 14.6 %collective-permute-start.1 = (f32[6,64,256]{2,1,0:T(8,128)S(1)}, f32[6,64,256]{2,1,0:T(8,128)}, u32[]{:S(2)}, u32[]{:S(2)}) collective-permute-start(f32[6,64,256]{2,1,0:T(8,128)S(1)} %get-tuple-element.1197.prev), channel_id=1, source_target_pairs={{8,0},{16,8},{24,16},{9,1},{17,9},{25,17},{10,2},{18,10},{26,18},{... | collective-permute-start | bytes 1179656 | tf_op jit(solution)/shard_map/while/body/eval_jaxpr/ppermute | solution.py:875
  121.7 14.0 %collective-permute-start = (f32[6,64,256]{2,1,0:T(8,128)}, f32[6,64,256]{2,1,0:T(8,128)S(1)}, u32[]{:S(2)}, u32[]{:S(2)}) collective-permute-start(f32[6,64,256]{2,1,0:T(8,128)} %get-tuple-element.1259), channel_id=1, source_target_pairs={{8,0},{16,8},{24,16},{9,1},{17,9},{25,17},{10,2},{18,10},{26,18},{... | collective-permute-start | bytes 1179656 | tf_op jit(solution)/shard_map/while/body/eval_jaxpr/ppermute | solution.py:871
  134.0 14.6 %collective-permute-start.1 = (f32[6,64,256]{2,1,0:T(8,128)S(1)}, f32[6,64,256]{2,1,0:T(8,128)}, u32[]{:S(2)}, u32[]{:S(2)}) collective-permute-start(f32[6,64,256]{2,1,0:T(8,128)S(1)} %get-tuple-element.1197.prev), channel_id=1, source_target_pairs={{8,0},{16,8},{24,16},{9,1},{17,9},{25,17},{10,2},{18,10},{26,18},{... | collective-permute-start | bytes 1179656 | tf_op jit(solution)/shard_map/while/body/eval_jaxpr/ppermute | solution.py:875
  148.6 14.1 %collective-permute-start = (f32[6,64,256]{2,1,0:T(8,128)}, f32[6,64,256]{2,1,0:T(8,128)S(1)}, u32[]{:S(2)}, u32[]{:S(2)}) collective-permute-start(f32[6,64,256]{2,1,0:T(8,128)} %get-tuple-element.1259), channel_id=1, source_target_pairs={{8,0},{16,8},{24,16},{9,1},{17,9},{25,17},{10,2},{18,10},{26,18},{... | collective-permute-start | bytes 1179656 | tf_op jit(solution)/shard_map/while/body/eval_jaxpr/ppermute | solution.py:871
  160.8 14.6 %collective-permute-start.1 = (f32[6,64,256]{2,1,0:T(8,128)S(1)}, f32[6,64,256]{2,1,0:T(8,128)}, u32[]{:S(2)}, u32[]{:S(2)}) collective-permute-start(f32[6,64,256]{2,1,0:T(8,128)S(1)} %get-tuple-element.1197.prev), channel_id=1, source_target_pairs={{8,0},{16,8},{24,16},{9,1},{17,9},{25,17},{10,2},{18,10},{26,18},{... | collective-permute-start | bytes 1179656 | tf_op jit(solution)/shard_map/while/body/eval_jaxpr/ppermute | solution.py:875
  175.4 14.1 %collective-permute-start = (f32[6,64,256]{2,1,0:T(8,128)}, f32[6,64,256]{2,1,0:T(8,128)S(1)}, u32[]{:S(2)}, u32[]{:S(2)}) collective-permute-start(f32[6,64,256]{2,1,0:T(8,128)} %get-tuple-element.1259), channel_id=1, source_target_pairs={{8,0},{16,8},{24,16},{9,1},{17,9},{25,17},{10,2},{18,10},{26,18},{... | collective-permute-start | bytes 1179656 | tf_op jit(solution)/shard_map/while/body/eval_jaxpr/ppermute | solution.py:871
  187.7 14.6 %collective-permute-start.1 = (f32[6,64,256]{2,1,0:T(8,128)S(1)}, f32[6,64,256]{2,1,0:T(8,128)}, u32[]{:S(2)}, u32[]{:S(2)}) collective-permute-start(f32[6,64,256]{2,1,0:T(8,128)S(1)} %get-tuple-element.1197.prev), channel_id=1, source_target_pairs={{8,0},{16,8},{24,16},{9,1},{17,9},{25,17},{10,2},{18,10},{26,18},{... | collective-permute-start | bytes 1179656 | tf_op jit(solution)/shard_map/while/body/eval_jaxpr/ppermute | solution.py:875
  202.3 14.1 %collective-permute-start = (f32[6,64,256]{2,1,0:T(8,128)}, f32[6,64,256]{2,1,0:T(8,128)S(1)}, u32[]{:S(2)}, u32[]{:S(2)}) collective-permute-start(f32[6,64,256]{2,1,0:T(8,128)} %get-tuple-element.1259), channel_id=1, source_target_pairs={{8,0},{16,8},{24,16},{9,1},{17,9},{25,17},{10,2},{18,10},{26,18},{... | collective-permute-start | bytes 1179656 | tf_op jit(solution)/shard_map/while/body/eval_jaxpr/ppermute | solution.py:871
  214.6 14.6 %collective-permute-start.1 = (f32[6,64,256]{2,1,0:T(8,128)S(1)}, f32[6,64,256]{2,1,0:T(8,128)}, u32[]{:S(2)}, u32[]{:S(2)}) collective-permute-start(f32[6,64,256]{2,1,0:T(8,128)S(1)} %get-tuple-element.1197.prev), channel_id=1, source_target_pairs={{8,0},{16,8},{24,16},{9,1},{17,9},{25,17},{10,2},{18,10},{26,18},{... | collective-permute-start | bytes 1179656 | tf_op jit(solution)/shard_map/while/body/eval_jaxpr/ppermute | solution.py:875
  229.2 14.1 %collective-permute-start = (f32[6,64,256]{2,1,0:T(8,128)}, f32[6,64,256]{2,1,0:T(8,128)S(1)}, u32[]{:S(2)}, u32[]{:S(2)}) collective-permute-start(f32[6,64,256]{2,1,0:T(8,128)} %get-tuple-element.1259), channel_id=1, source_target_pairs={{8,0},{16,8},{24,16},{9,1},{17,9},{25,17},{10,2},{18,10},{26,18},{... | collective-permute-start | bytes 1179656 | tf_op jit(solution)/shard_map/while/body/eval_jaxpr/ppermute | solution.py:871
  241.4 14.6 %collective-permute-start.1 = (f32[6,64,256]{2,1,0:T(8,128)S(1)}, f32[6,64,256]{2,1,0:T(8,128)}, u32[]{:S(2)}, u32[]{:S(2)}) collective-permute-start(f32[6,64,256]{2,1,0:T(8,128)S(1)} %get-tuple-element.1197.prev), channel_id=1, source_target_pairs={{8,0},{16,8},{24,16},{9,1},{17,9},{25,17},{10,2},{18,10},{26,18},{... | collective-permute-start | bytes 1179656 | tf_op jit(solution)/shard_map/while/body/eval_jaxpr/ppermute | solution.py:875
  264.1 10.1 %collective-permute-start.4 = (f32[4,408,512]{2,1,0:T(8,128)S(1)}, f32[4,408,512]{2,1,0:T(8,128)}, u32[]{:S(2)}, u32[]{:S(2)}) collective-permute-start(f32[4,408,512]{2,1,0:T(8,128)S(1)} %get-tuple-element.864), channel_id=1, source_target_pairs={{0,1},{1,0},{2,3},{3,2},{4,5},{5,4},{6,7},{7,6},{8,9},{9,8},{10,11... | collective-permute-start | bytes 10027016 | tf_op jit(solution)/shard_map/ppermute | solution.py:791
  264.2 16.7 %collective-permute-start.3 = (f32[4,408,512]{2,1,0:T(8,128)}, f32[4,408,512]{2,1,0:T(8,128)}, u32[]{:S(2)}, u32[]{:S(2)}) collective-permute-start(f32[4,408,512]{2,1,0:T(8,128)} %get-tuple-element.862), channel_id=1, source_target_pairs={{0,1},{1,0},{2,3},{3,2},{4,5},{5,4},{6,7},{7,6},{8,9},{9,8},{10,11... | collective-permute-start | bytes 10027016 | tf_op jit(solution)/shard_map/ppermute | solution.py:791
  274.2 24.4 %copy-start.19 = (f32[4,408,512]{2,1,0:T(8,128)S(1)}, f32[4,408,512]{2,1,0:T(8,128)}, u32[]{:S(2)}) copy-start(f32[4,408,512]{2,1,0:T(8,128)} %get-tuple-element.861) | copy-start | bytes 10027012
  277.1 21.5 %collective-permute-start.12 = (f32[408,512]{1,0:T(8,128)S(1)}, f32[408,512]{1,0:T(8,128)S(1)}, u32[]{:S(2)}, u32[]{:S(2)}) collective-permute-start(f32[408,512]{1,0:T(8,128)S(1)} %get-tuple-element.961), channel_id=1, source_target_pairs={{0,4},{1,5},{2,6},{3,7},{4,0},{5,1},{6,2},{7,3},{8,12},{9,13},{10,... | collective-permute-start | bytes 2506760 | tf_op jit(solution)/shard_map/ppermute | solution.py:791
  278.8 36.9 %collective-permute-start.11 = (f32[408,512]{1,0:T(8,128)S(1)}, f32[408,512]{1,0:T(8,128)S(1)}, u32[]{:S(2)}, u32[]{:S(2)}) collective-permute-start(f32[408,512]{1,0:T(8,128)S(1)} %get-tuple-element.960), channel_id=1, source_target_pairs={{0,4},{1,5},{2,6},{3,7},{4,0},{5,1},{6,2},{7,3},{8,12},{9,13},{10,... | collective-permute-start | bytes 2506760 | tf_op jit(solution)/shard_map/ppermute | solution.py:791
  279.2 36.5 %collective-permute-start.6 = (f32[408,512]{1,0:T(8,128)S(1)}, f32[408,512]{1,0:T(8,128)S(1)}, u32[]{:S(2)}, u32[]{:S(2)}) collective-permute-start(f32[408,512]{1,0:T(8,128)S(1)} %get-tuple-element.962), channel_id=1, source_target_pairs={{0,2},{1,3},{2,0},{3,1},{4,6},{5,7},{6,4},{7,5},{8,10},{9,11},{10,... | collective-permute-start | bytes 2506760 | tf_op jit(solution)/shard_map/ppermute | solution.py:791
  300.0 21.6 %collective-permute-start.13 = (f32[408,512]{1,0:T(8,128)S(1)}, f32[408,512]{1,0:T(8,128)S(1)}, u32[]{:S(2)}, u32[]{:S(2)}) collective-permute-start(f32[408,512]{1,0:T(8,128)S(1)} %fusion.2), channel_id=1, source_target_pairs={{0,2},{1,3},{2,0},{3,1},{4,6},{5,7},{6,4},{7,5},{8,10},{9,11},{10,... | collective-permute-start | bytes 2506760 | tf_op jit(solution)/shard_map/ppermute | solution.py:791
  301.7 37.8 %collective-permute-start.5 = (f32[408,512]{1,0:T(8,128)S(1)}, f32[408,512]{1,0:T(8,128)S(1)}, u32[]{:S(2)}, u32[]{:S(2)}) collective-permute-start(f32[408,512]{1,0:T(8,128)S(1)} %get-tuple-element.963), channel_id=1, source_target_pairs={{0,2},{1,3},{2,0},{3,1},{4,6},{5,7},{6,4},{7,5},{8,10},{9,11},{10,... | collective-permute-start | bytes 2506760 | tf_op jit(solution)/shard_map/ppermute | solution.py:791
  323.7 59.2 %copy-start.13 = (f32[7,4,64,256]{3,2,1,0:T(8,128)S(1)}, f32[7,4,64,256]{3,2,1,0:T(8,128)}, u32[]{:S(2)}) copy-start(f32[7,4,64,256]{3,2,1,0:T(8,128)} %get-tuple-element.875) | copy-start | bytes 5505028
  323.7 21.6 %collective-permute-start.7 = (f32[408,512]{1,0:T(8,128)S(1)}, f32[408,512]{1,0:T(8,128)S(1)}, u32[]{:S(2)}, u32[]{:S(2)}) collective-permute-start(f32[408,512]{1,0:T(8,128)S(1)} %get-tuple-element.959), channel_id=1, source_target_pairs={{0,4},{1,5},{2,6},{3,7},{4,0},{5,1},{6,2},{7,3},{8,12},{9,13},{10,... | collective-permute-start | bytes 2506760 | tf_op jit(solution)/shard_map/ppermute | solution.py:791
  325.5 32.0 %collective-permute-start.14 = (f32[408,512]{1,0:T(8,128)S(1)}, f32[408,512]{1,0:T(8,128)S(1)}, u32[]{:S(2)}, u32[]{:S(2)}) collective-permute-start(f32[408,512]{1,0:T(8,128)S(1)} %get-tuple-element.958.refs_5_), channel_id=1, source_target_pairs={{0,2},{1,3},{2,0},{3,1},{4,6},{5,7},{6,4},{7,5},{8,10},{9,11},{10,... | collective-permute-start | bytes 2506760 | tf_op jit(solution)/shard_map/ppermute | solution.py:791
  327.0 36.3 %collective-permute-start.15 = (f32[408,512]{1,0:T(8,128)S(1)}, f32[408,512]{1,0:T(8,128)S(1)}, u32[]{:S(2)}, u32[]{:S(2)}) collective-permute-start(f32[408,512]{1,0:T(8,128)S(1)} %get-tuple-element.958.refs_5_), channel_id=1, source_target_pairs={{0,4},{1,5},{2,6},{3,7},{4,0},{5,1},{6,2},{7,3},{8,12},{9,13},{10,... | collective-permute-start | bytes 2506760 | tf_op jit(solution)/shard_map/ppermute | solution.py:791
  327.5 37.4 %collective-permute-start.21 = (f32[408,512]{1,0:T(8,128)S(1)}, f32[408,512]{1,0:T(8,128)S(1)}, u32[]{:S(2)}, u32[]{:S(2)}) collective-permute-start(f32[408,512]{1,0:T(8,128)S(1)} %get-tuple-element.958.refs_5_), channel_id=1, source_target_pairs={{0,1},{1,0},{2,3},{3,2},{4,5},{5,4},{6,7},{7,6},{8,9},{9,8},{10,11... | collective-permute-start | bytes 2506760 | tf_op jit(solution)/shard_map/ppermute | solution.py:791
  346.9 34.4 %collective-permute-start.8 = (f32[408,512]{1,0:T(8,128)S(1)}, f32[408,512]{1,0:T(8,128)}, u32[]{:S(2)}, u32[]{:S(2)}) collective-permute-start(f32[408,512]{1,0:T(8,128)S(1)} %fusion.13.refs_1_), channel_id=1, source_target_pairs={{0,4},{1,5},{2,6},{3,7},{4,0},{5,1},{6,2},{7,3},{8,12},{9,13},{10,... | collective-permute-start | bytes 2506760 | tf_op jit(solution)/shard_map/ppermute | solution.py:791
  348.6 40.0 %collective-permute-start.9 = (f32[408,512]{1,0:T(8,128)S(1)}, f32[408,512]{1,0:T(8,128)}, u32[]{:S(2)}, u32[]{:S(2)}) collective-permute-start(f32[408,512]{1,0:T(8,128)S(1)} %fusion.13.refs_1_), channel_id=1, source_target_pairs={{0,2},{1,3},{2,0},{3,1},{4,6},{5,7},{6,4},{7,5},{8,10},{9,11},{10,... | collective-permute-start | bytes 2506760 | tf_op jit(solution)/shard_map/ppermute | solution.py:791
  357.4 31.2 %collective-permute-start.17 = (f32[408,512]{1,0:T(8,128)S(1)}, f32[408,512]{1,0:T(8,128)}, u32[]{:S(2)}, u32[]{:S(2)}) collective-permute-start(f32[408,512]{1,0:T(8,128)S(1)} %fusion.13.refs_1_), channel_id=1, source_target_pairs={{0,1},{1,0},{2,3},{3,2},{4,5},{5,4},{6,7},{7,6},{8,9},{9,8},{10,11... | collective-permute-start | bytes 2506760 | tf_op jit(solution)/shard_map/ppermute | solution.py:791
  363.2 29.9 %collective-permute-start.16 = (f32[408,512]{1,0:T(8,128)S(1)}, f32[408,512]{1,0:T(8,128)}, u32[]{:S(2)}, u32[]{:S(2)}) collective-permute-start(f32[408,512]{1,0:T(8,128)S(1)} %collective-permute-done.14.refs_6_), channel_id=1, source_target_pairs={{0,4},{1,5},{2,6},{3,7},{4,0},{5,1},{6,2},{7,3},{8,12},{9,13},{10,... | collective-permute-start | bytes 2506760 | tf_op jit(solution)/shard_map/ppermute | solution.py:791
  364.9 18.1 %copy-start.20 = (f32[408,512]{1,0:T(8,128)}, f32[408,512]{1,0:T(8,128)S(1)}, u32[]{:S(2)}) copy-start(f32[408,512]{1,0:T(8,128)S(1)} %collective-permute-done.21.refs_13_) | copy-start | bytes 2506756
  364.9 28.3 %collective-permute-start.22 = (f32[408,512]{1,0:T(8,128)S(1)}, f32[408,512]{1,0:T(8,128)}, u32[]{:S(2)}, u32[]{:S(2)}) collective-permute-start(f32[408,512]{1,0:T(8,128)S(1)} %collective-permute-done.14.refs_6_), channel_id=1, source_target_pairs={{0,1},{1,0},{2,3},{3,2},{4,5},{5,4},{6,7},{7,6},{8,9},{9,8},{10,11... | collective-permute-start | bytes 2506760 | tf_op jit(solution)/shard_map/ppermute | solution.py:791
  381.2 12.8 %collective-permute-start.10 = (f32[408,512]{1,0:T(8,128)}, f32[408,512]{1,0:T(8,128)}, u32[]{:S(2)}, u32[]{:S(2)}) collective-permute-start(f32[408,512]{1,0:T(8,128)} %collective-permute-done.8.refs_2_), channel_id=1, source_target_pairs={{0,2},{1,3},{2,0},{3,1},{4,6},{5,7},{6,4},{7,5},{8,10},{9,11},{10,... | collective-permute-start | bytes 2506760 | tf_op jit(solution)/shard_map/ppermute | solution.py:791
  388.6 5.5 collective-permute-start.23
  388.7 5.4 collective-permute-start.18
  393.2 2.6 collective-permute-start.19
  393.2 3.8 collective-permute-start.24
  394.1 4.1 collective-permute-start.20
  (93 other events, 778.7 us)
Sparse Core Ops, SparseCore 0:
  388.7 72.5 all-reduce.1
